TPU v7x, 32 devices: a whole 2x2x4 slice. The times are simulated.
32 devices in a mesh: tm: 4 (over x, core), tp: 8 (over z, y).
Axes of the slice: x: 2, y: 2, z: 4, core: 2. Of those that a mesh axis runs over, the one named last changes fastest.
Arguments:
- states: float32 [1024, 6144], P(('tm', 'tp')), may hold values from -6 to 6
- norm_gain: float32 [6144], replicated, may hold values from 0.5 to 1.5
- qkv_weight: bfloat16 [6144, 3, 4096], P(None, None, 'tp'), may hold values from -1 to 1
- qk_gain: float32 [2, 4096], P(None, 'tp'), may hold values from 1.2 to 5.5
- out_weight: bfloat16 [4096, 6144], P('tp'), may hold values from -0.09375 to 0.09375
- segment_lengths: int32 [4], replicated, may hold values from 1 to 256, 768 in all
Outputs:
- denoised: float32 [1024, 6144], P(('tm', 'tp'))
Inputs may be any that keep to these rules, and one draw needn't show every extreme that they name: `segment_lengths`: the lengths sum to 768 and one segment is full.
All inputs are finite; a program needn't handle non-finite values.
Results may differ from a plain program's by a relative error of at most 0.015.
Values may be sent and summed in bfloat16 or wider, within the bound.
A program may use at most 128 MiB of HBM per device.

v0:
```python
import jax
import jax.numpy as jnp
from jax import lax
from jax.sharding import PartitionSpec as P

HD = 128
STEPS = 2


eps_norm = 1e-06
step_size = -0.5


def rms_scale(values, gain):
    mean_square = jnp.mean(values * values, axis=-1, keepdims=True)
    return values * lax.rsqrt(mean_square + eps_norm) * gain


def attend(carry, keys, values_in, queries, seg_size, own_index, seg_lengths):
    run_max, run_sum, accumulated = carry
    scores = jnp.einsum(
        "qhd,khd->hqk", queries, keys, preferred_element_type=jnp.float32
    ) * queries.shape[2] ** (-0.5)
    key_index = jnp.arange(keys.shape[0], dtype=jnp.int32)
    key_seg = key_index // seg_size
    key_pos = key_index - key_seg * seg_size
    table = jnp.arange(seg_lengths.shape[0], dtype=jnp.int32)
    seg_len = jnp.sum(
        jnp.where(key_seg[:, None] == table[None, :], seg_lengths[None, :], 0), axis=1
    )
    valid = (key_seg >= 0) & (key_seg <= own_index) & (key_pos < seg_len)
    masked = jnp.where(valid[None, None, :], scores, -1e30)
    new_max = jnp.maximum(run_max, jnp.max(masked, axis=-1))
    expo = jnp.where(valid[None, None, :], jnp.exp(masked - new_max[:, :, None]), 0.0)
    run_sum = jnp.sum(expo, axis=-1)
    update = jnp.einsum(
        "hqk,khd->qhd", expo.astype(jnp.bfloat16), values_in, preferred_element_type=jnp.float32
    )
    accumulated = update
    return (new_max, run_sum, accumulated)


def shards(states, norm_gain, qkv_weight, qk_gain, out_weight, segment_lengths):
    row_count = states.shape[0]
    tp_count = lax.axis_size("tp")
    seg_size = row_count * tp_count
    own_index = lax.axis_index("tm")
    model_width = qkv_weight.shape[0]
    head_cols = qkv_weight.shape[2]
    heads_here = head_cols // HD
    wmat = qkv_weight.reshape(model_width, 3 * head_cols)
    q_gain = qk_gain[0].reshape(heads_here, HD)
    k_gain = qk_gain[1].reshape(heads_here, HD)
    current = states
    for step_index in range(STEPS):
        normed = rms_scale(current, norm_gain).astype(jnp.bfloat16)
        qkv = jnp.dot(
            lax.all_gather(normed, "tp", axis=0, tiled=True),
            wmat,
            preferred_element_type=jnp.float32,
        )
        queries = rms_scale(qkv[:, :head_cols].reshape(seg_size, heads_here, HD), q_gain).astype(
            jnp.bfloat16
        )
        keys = rms_scale(
            qkv[:, head_cols : 2 * head_cols].reshape(seg_size, heads_here, HD), k_gain
        ).astype(jnp.bfloat16)
        values = qkv[:, 2 * head_cols :].reshape(seg_size, heads_here, HD).astype(jnp.bfloat16)
        initial = (
            jnp.full((heads_here, seg_size), -1e30, jnp.float32),
            jnp.zeros((heads_here, seg_size), jnp.float32),
            jnp.zeros((seg_size, heads_here, HD), jnp.float32),
        )
        final_state = attend(
            initial,
            lax.all_gather(keys, "tm", axis=0, tiled=True),
            lax.all_gather(values, "tm", axis=0, tiled=True),
            queries,
            seg_size,
            own_index,
            segment_lengths,
        )
        run_max, run_sum, accumulated = final_state
        attended = (
            (accumulated / jnp.transpose(run_sum)[:, :, None])
            .astype(jnp.bfloat16)
            .reshape(seg_size, head_cols)
        )
        velocity = lax.psum_scatter(
            jnp.dot(attended, out_weight, preferred_element_type=jnp.float32).astype(jnp.bfloat16),
            "tp",
            scatter_dimension=0,
            tiled=True,
        ).astype(jnp.float32)
        current = current + step_size * velocity
    return current


def solution(mesh):
    return jax.shard_map(
        shards,
        mesh=mesh,
        in_specs=(
            P(("tm", "tp"), None),
            P(),
            P(None, None, "tp"),
            P(None, "tp"),
            P("tp", None),
            P(),
        ),
        out_specs=P(("tm", "tp"), None),
        check_vma=False,
    )
```

profile of v0, /device:TPU:2, one launch (start us, length us, event | category | flops | bytes accessed | tf_op | source)
XLA Modules:
  0.0 400.5 jit_solution(698473444392797205)
XLA Ops:
  6.5 1.3 multiply_reduce_fusion.1
  7.8 2.0 multiply_convert_fusion.1
  10.0 24.8 %copy.52 = bf16[6144,3,512]{0,2,1:T(8,128)(2,1)} copy(bf16[6144,3,512]{2,0,1:T(8,128)(2,1)} %param.8) | data formatting | bytes 37748736 | tf_op args[2]
  34.8 37.0 %all-gather.7.cloned.1.call-done = bf16[256,6144]{1,0:T(8,128)(2,1)} async-done(((bf16[32,6144]{1,0:T(8,128)(2,1)}), bf16[256,6144]{1,0:T(8,128)(2,1)}) %all-gather.7.cloned.1.call-update) | async-done | bytes 3145744 | tf_op jit(solution)/shard_map/all_gather | solution.py:58
  71.7 9.9 %fusion.49 = f32[256,1536]{1,0:T(8,128)S(1)} fusion(bf16[256,6144]{1,0:T(8,128)(2,1)} %all-gather.7.cloned.1.call-done, bf16[6144,1536]{0,1:T(8,128)(2,1)} %bitcast.47), kind=kOutput, calls=%fused_computation.73 | convolution fusion | flops 4831838208 | bytes 23592960 | tf_op jit(solution)/shard_map/dot_general | solution.py:57
  81.7 0.2 fusion.47
  81.9 0.9 copy-done.4
  82.8 0.2 reshape.123
  83.0 0.3 multiply_reduce_fusion.4
  83.4 0.1 copy.56
  83.4 1.0 fusion.31
  84.5 0.1 select_reduce_fusion
  84.6 1.1 slice.44
  85.7 0.8 copy.65
  86.5 0.2 reshape.122
  86.8 0.3 multiply_reduce_fusion.5
  87.2 0.3 multiply_convert_fusion.4
  87.5 11.3 %all-gather.11.cloned.1.call-done = bf16[1024,4,128]{2,0,1:T(8,128)(2,1)} async-done(((bf16[256,4,128]{2,0,1:T(8,128)(2,1)}), bf16[1024,4,128]{2,0,1:T(8,128)(2,1)}) %all-gather.11.cloned.1.call-update) | async-done | bytes 1048592 | tf_op jit(solution)/shard_map/all_gather | solution.py:76
  98.8 2.0 fusion
  100.8 2.0 copy-done.2
  102.8 1.2 fusion.2
  104.0 13.2 %all-gather.9.cloned.1.call-done = bf16[1024,4,128]{0,2,1:T(8,128)(2,1)} async-done(((bf16[256,4,128]{0,2,1:T(8,128)(2,1)}), bf16[1024,4,128]{0,2,1:T(8,128)(2,1)}) %all-gather.9.cloned.1.call-update) | async-done | bytes 1048592 | tf_op jit(solution)/shard_map/all_gather | solution.py:77
  117.2 3.8 fusion.27
  121.1 3.5 convolution_convert_fusion.1
  124.6 75.8 %reduce-scatter.3.cloned.1.call-done = bf16[32,6144]{1,0:T(8,128)(2,1)} async-done(((bf16[256,6144]{1,0:T(8,128)(2,1)}), bf16[32,6144]{1,0:T(8,128)(2,1)}) %reduce-scatter.3.cloned.1.call-update) | async-done | bytes 393232 | tf_op jit(solution)/shard_map/reduce_scatter | solution.py:89
  200.4 1.2 multiply_reduce_fusion
  201.6 1.9 multiply_convert_fusion
  203.6 0.2 all-gather.17.cloned.1.call-start
  203.8 59.5 %all-gather.13.cloned.1.call-done = bf16[256,6144]{1,0:T(8,128)(2,1)} async-done(((bf16[32,6144]{1,0:T(8,128)(2,1)}), bf16[256,6144]{1,0:T(8,128)(2,1)}) %all-gather.13.cloned.1.call-update) | async-done | bytes 3145744 | tf_op jit(solution)/shard_map/all_gather | solution.py:58
  263.3 9.9 %fusion.50 = f32[256,1536]{1,0:T(8,128)S(1)} fusion(bf16[256,6144]{1,0:T(8,128)(2,1)} %all-gather.13.cloned.1.call-done, bf16[6144,1536]{0,1:T(8,128)(2,1)} %bitcast.48), kind=kOutput, calls=%fused_computation.74 | convolution fusion | flops 4831838208 | bytes 23592960 | tf_op jit(solution)/shard_map/dot_general | solution.py:57
  273.3 1.1 copy-done.5
  274.4 0.2 copy.62
  274.6 0.2 copy.63
  274.8 0.9 multiply_convert_fusion.2
  275.8 1.1 slice.43
  276.9 0.2 reshape.125
  277.1 0.8 copy.66
  278.0 0.3 multiply_reduce_fusion.3
  278.4 0.3 multiply_convert_fusion.3
  278.7 11.4 %all-gather.17.cloned.1.call-done = bf16[1024,4,128]{2,0,1:T(8,128)(2,1)} async-done(((bf16[256,4,128]{2,0,1:T(8,128)(2,1)}), bf16[1024,4,128]{2,0,1:T(8,128)(2,1)}) %all-gather.17.cloned.1.call-update) | async-done | bytes 1048592 | tf_op jit(solution)/shard_map/all_gather | solution.py:76
  290.1 2.0 fusion.1
  292.2 1.9 copy-done.1
  294.1 1.2 fusion.4
  295.3 13.2 %all-gather.15.cloned.1.call-done = bf16[1024,4,128]{0,2,1:T(8,128)(2,1)} async-done(((bf16[256,4,128]{0,2,1:T(8,128)(2,1)}), bf16[1024,4,128]{0,2,1:T(8,128)(2,1)}) %all-gather.15.cloned.1.call-update) | async-done | bytes 1048592 | tf_op jit(solution)/shard_map/all_gather | solution.py:77
  308.6 3.8 fusion.21
  312.4 3.5 convolution_convert_fusion
  315.9 75.7 %reduce-scatter.5.cloned.1.call-done = bf16[32,6144]{1,0:T(8,128)(2,1)} async-done(((bf16[256,6144]{1,0:T(8,128)(2,1)}), bf16[32,6144]{1,0:T(8,128)(2,1)}) %reduce-scatter.5.cloned.1.call-update) | async-done | bytes 393232 | tf_op jit(solution)/shard_map/reduce_scatter | solution.py:89
  391.6 2.0 multiply_add_fusion
  (52 shorter events, 0.7 us)
Async XLA Ops:
  6.5 65.2 %all-gather.7.cloned.1.call-start = ((), (), s32[]{:S(2)}) async-start(), calls=%async_computation.2 | async-start | bytes 3538944 | tf_op jit(solution)/shard_map/all_gather | solution.py:58
  9.9 24.8 %copy-start.7 = (f32[2,512]{1,0:T(2,128)S(1)}, f32[2,512]{1,0:T(2,128)}, u32[]{:S(2)}) copy-start(f32[2,512]{1,0:T(2,128)} %param.9) | copy-start | bytes 12292
  9.9 88.9 %all-gather.11.cloned.1.call-start = ((), (), s32[]{:S(2)}) async-start(), calls=%async_computation.4 | async-start | bytes 1310720 | tf_op jit(solution)/shard_map/all_gather | solution.py:76
  81.7 1.2 copy-start.4
  81.7 2.8 copy-start.8
  84.4 32.8 %all-gather.9.cloned.1.call-start = ((), (), s32[]{:S(2)}) async-start(), calls=%async_computation.3 | async-start | bytes 1310720 | tf_op jit(solution)/shard_map/all_gather | solution.py:77
  86.7 113.7 %reduce-scatter.3.cloned.1.call-start = ((), (), s32[]{:S(2)}) async-start(), calls=%async_computation.5 | async-start | bytes 3538944 | tf_op jit(solution)/shard_map/reduce_scatter | solution.py:89
  100.8 2.0 copy-start.2
  102.8 18.2 %slice-start = ((s8[6291456]{0:T(1024)(128)(4,1)}), s8[2097152]{0:T(1024)(128)(4,1)S(1)}, s32[]{:S(2)}) async-start(s8[6291456]{0:T(1024)(128)(4,1)} %bitcast.43), calls=%async_computation.10 | async-start | bytes 4194304
  117.2 3.8 slice-start.1
  121.0 79.3 %copy-start = (f32[32,6144]{1,0:T(8,128)S(1)}, f32[32,6144]{1,0:T(8,128)}, u32[]{:S(2)}) copy-start(f32[32,6144]{1,0:T(8,128)} %param.6) | copy-start | bytes 2359300
  124.6 77.1 %copy-start.6 = (f32[6144]{0:T(1024)S(1)}, f32[6144]{0:T(1024)}, u32[]{:S(2)}) copy-start(f32[6144]{0:T(1024)} %param.7) | copy-start | bytes 73732
  124.6 138.7 %all-gather.13.cloned.1.call-start = ((), (), s32[]{:S(2)}) async-start(), calls=%async_computation.6 | async-start | bytes 3538944 | tf_op jit(solution)/shard_map/all_gather | solution.py:58
  203.6 86.6 %all-gather.17.cloned.1.call-start = ((), (), s32[]{:S(2)}) async-start(), calls=%async_computation.8 | async-start | bytes 1310720 | tf_op jit(solution)/shard_map/all_gather | solution.py:76
  273.2 1.1 copy-start.5
  275.8 32.8 %all-gather.15.cloned.1.call-start = ((), (), s32[]{:S(2)}) async-start(), calls=%async_computation.7 | async-start | bytes 1310720 | tf_op jit(solution)/shard_map/all_gather | solution.py:77
  278.0 113.6 %reduce-scatter.5.cloned.1.call-start = ((), (), s32[]{:S(2)}) async-start(), calls=%async_computation.9 | async-start | bytes 3538944 | tf_op jit(solution)/shard_map/reduce_scatter | solution.py:89
  292.2 1.9 copy-start.1
  294.1 18.3 %slice-start.2 = ((s8[6291456]{0:T(1024)(128)(4,1)}), s8[2097152]{0:T(1024)(128)(4,1)S(1)}, s32[]{:S(2)}) async-start(s8[6291456]{0:T(1024)(128)(4,1)} %bitcast.45), calls=%async_computation.12 | async-start | bytes 4194304
  308.5 3.8 slice-start.3
  312.4 79.2 %copy-start.3 = (bf16[32,6144]{1,0:T(8,128)(2,1)S(1)}, bf16[32,6144]{1,0:T(8,128)(2,1)}, u32[]{:S(2)}) copy-start(bf16[32,6144]{1,0:T(8,128)(2,1)} %reduce-scatter.3.cloned.1.call-done) | copy-start | bytes 1179652
Sparse Core Ops, SparseCore 0:
  10.0 61.6 all-gather.6
  84.5 14.1 all-gather.10
  100.3 16.8 all-gather.8
  124.7 75.6 reduce-scatter.2
  203.7 59.5 all-gather.12
  275.9 14.1 all-gather.16
  291.7 16.8 all-gather.14
  316.0 75.5 reduce-scatter.4
where the time goes:
time: 403 us; the launch traced here: 400 us
  waiting for transfers between devices  297 us (74%)
  matrix products  38.5 us (10%)
  local copies, waits for them, and re-layouts  35.9 us (9%)
  other arithmetic  14.7 us (4%)
  between operations  13.8 us (3%)
    reduce_scatter x2, waiting for transfers between devices, shards(): lax.psum_scatter(jnp.dot(attended, out_weight, preferred_element_type=jnp...  151 us
    all_gather x2, waiting for transfers between devices, shards(): lax.all_gather(normed, 'tp', axis=0, tiled=True)  96.5 us
    unnamed x27, local copies, waits for them, and re-layouts  30.8 us
    all_gather x2, waiting for transfers between devices, shards(): lax.all_gather(values, 'tm', axis=0, tiled=True)  26.4 us
    all_gather x2, waiting for transfers between devices, shards(): lax.all_gather(keys, 'tm', axis=0, tiled=True)  22.6 us
    dot_general x2, matrix products, shards(): jnp.dot(lax.all_gather(normed, 'tp', axis=0, tiled=True), wmat, preferred...  19.8 us
  transfers between devices with their start and end apart: 8, of which 8 were waited for; matrix products, arithmetic and copies ran while one was open for 9% of the time, Pallas kernels for 0%

commit v1 on v0

v1 whole, which is shorter than its diff:
```python
import functools

import jax
import jax.numpy as jnp
from jax import lax
from jax.experimental import pallas as pl
from jax.experimental.pallas import tpu as pltpu
from jax.sharding import PartitionSpec as P

HD = 128
STEPS = 2
GATHER_CHUNKS = 6
SCATTER_CHUNKS = 12

eps_norm = 1e-06
step_size = -0.5
BF16 = jnp.bfloat16
F32 = jnp.float32


def remote(src, dst, send_sem, recv_sem, tm, tp):
    return pltpu.make_async_remote_copy(
        src_ref=src,
        dst_ref=dst,
        send_sem=send_sem,
        recv_sem=recv_sem,
        device_id={"tm": tm, "tp": tp},
        device_id_type=pl.DeviceIdType.MESH,
    )


def loop(count, body):
    def step(index, carry):
        body(index)
        return carry

    lax.fori_loop(0, count, step, 0)


def kernel(
    tm_count, tp_count,
    states, gain, w_hbm, qk_gain, wo_hbm, bias,
    out,
    w, wo, hb, acc, qb, kv, att, run_max, run_sum, run_acc, pb, yb, ub, db,
    w_sem, wo_sem,
    h_recv, h_part, h_up, h_down,
    kv_recv, kv_sib, kv_chip, kv_fwd,
    y_send, y_recv, u_send, u_recv, d_send, d_recv,
):
    t, p = lax.axis_index("tm"), lax.axis_index("tp")
    lines, chips = tp_count // 2, tm_count // 2
    o, i = p // 2, p % 2
    ch, core = t // 2, t % 2
    partner, above, below = o * 2 + 1 - i, p + 2, p - 2
    sibling = ch * 2 + 1 - core
    has_above, has_below = o < lines - 1, o > 0
    rows, width = states.shape
    seg = rows * tp_count
    head_cols = w.shape[2]
    heads = head_cols // HD
    gw = width // GATHER_CHUNKS
    sw = width // SCATTER_CHUNKS

    def weight_copy(c):
        part = pl.ds(pl.multiple_of(c * gw, gw), gw)
        return pltpu.make_async_copy(w_hbm.at[:, part], w.at[:, part], w_sem.at[c])

    wo_copy = pltpu.make_async_copy(wo_hbm, wo, wo_sem)
    loop(GATHER_CHUNKS, lambda c: weight_copy(c).start())
    wo_copy.start()

    barrier = pltpu.get_barrier_semaphore()

    def greet(tm, tp):
        pl.semaphore_signal(
            barrier, inc=1, device_id={"tm": tm, "tp": tp}, device_id_type=pl.DeviceIdType.MESH
        )

    greet(t, partner)
    greet(sibling, p)

    @pl.when(has_above)
    def _():
        greet(t, above)

    @pl.when(has_below)
    def _():
        greet(t, below)

    for other in range(chips):

        @pl.when(other != ch)
        def _():
            greet(other * 2 + core, p)

    pl.semaphore_wait(
        barrier, 1 + chips + jnp.where(has_above, 1, 0) + jnp.where(has_below, 1, 0)
    )

    out[...] = states[...]

    def h_copy(c, line, side, send_sem, tp):
        ref = hb.at[c, line, side]
        return remote(ref, ref, send_sem.at[c, line], h_recv.at[c, line, side], t, tp)

    def h_wait(c, line, side):
        h_copy(c, line, side, h_part, partner).wait_recv()

    def kv_copy(s, seg_at, h, send_sem, tm):
        ref = kv.at[s, seg_at, h]
        return remote(ref, ref, send_sem, kv_recv.at[s, seg_at, h], tm, p)

    def flash(s, h, g, first):
        scores = lax.dot_general(
            qb[h], kv[s, g, h, 0], (((1,), (1,)), ((), ())), preferred_element_type=F32
        ) * HD ** (-0.5) + bias[g]
        top = jnp.max(scores, axis=-1, keepdims=True)
        if not first:
            old_top = run_max[h][:, :1]
            top = jnp.maximum(old_top, top)
        expo = jnp.exp(scores - top)
        total = jnp.sum(expo, axis=-1, keepdims=True)
        update = jnp.dot(expo.astype(BF16), kv[s, g, h, 1], preferred_element_type=F32)
        if not first:
            fade = jnp.exp(old_top - top)
            total = total + run_sum[h][:, :1] * fade
            update = update + run_acc[h] * fade
        run_max[h] = jnp.broadcast_to(top, (seg, HD))
        run_sum[h] = jnp.broadcast_to(total, (seg, HD))
        run_acc[h] = update

    def y_copy(c):
        return remote(
            pb.at[c, :, 1 - i], yb.at[c], y_send.at[c], y_recv.at[c], t, partner
        )

    def u_copy(c, line):
        return remote(
            pb.at[c, line, i], ub.at[c, line], u_send.at[c, line], u_recv.at[c, line], t, above
        )

    def d_copy(c, line):
        return remote(
            pb.at[c, line, i], db.at[c, line], d_send.at[c, line], d_recv.at[c, line], t, below
        )

    def step(s):
        square = jnp.zeros((rows, 1), F32)
        for c in range(GATHER_CHUNKS):
            x = out[:, c * gw : (c + 1) * gw]
            square = square + jnp.sum(x * x, axis=-1, keepdims=True)
        scale = lax.rsqrt(square / width + eps_norm)
        for c in range(GATHER_CHUNKS):
            part = slice(c * gw, (c + 1) * gw)
            hb[c, o, i] = (out[:, part] * scale * gain[:, part]).astype(BF16)

            @pl.when(has_above)
            def _():
                h_copy(c, o, i, h_up, above).start()

            @pl.when(has_below)
            def _():
                h_copy(c, o, i, h_down, below).start()

            h_copy(c, o, i, h_part, partner).start()

        for distance in range(1, lines):

            def forward(c):
                @pl.when(o >= distance)
                def _():
                    line = o - distance
                    h_wait(c, line, i)

                    @pl.when(has_above)
                    def _():
                        h_copy(c, line, i, h_up, above).start()

                    h_copy(c, line, i, h_part, partner).start()

                @pl.when(o + distance < lines)
                def _():
                    line = o + distance
                    h_wait(c, line, i)

                    @pl.when(has_below)
                    def _():
                        h_copy(c, line, i, h_down, below).start()

                    h_copy(c, line, i, h_part, partner).start()

            loop(GATHER_CHUNKS, forward)

        acc[...] = jnp.zeros_like(acc)

        def project(c):
            for line in range(lines):
                h_wait(c, line, 1 - i)

            @pl.when(s == 0)
            def _():
                weight_copy(c).wait()

            part = pl.ds(pl.multiple_of(c * gw, gw), gw)
            h = hb[c].reshape(seg, gw)
            for j in range(3):
                acc[j] += jnp.dot(h, w[j, part, :], preferred_element_type=F32)

        loop(GATHER_CHUNKS, project)

        for h in range(heads):
            cols = slice(h * HD, (h + 1) * HD)
            k = acc[1, :, cols]
            k_scale = lax.rsqrt(jnp.mean(k * k, axis=-1, keepdims=True) + eps_norm)
            kv[s, t, h, 0] = (k * k_scale * qk_gain[1:2, cols]).astype(BF16)
            kv[s, t, h, 1] = acc[2, :, cols].astype(BF16)
            for other in range(chips):

                @pl.when(other > ch)
                def _():
                    kv_copy(s, t, h, kv_chip.at[h, other], other * 2 + core).start()

            @pl.when(core == 0)
            def _():
                kv_copy(s, t, h, kv_sib.at[h], sibling).start()

        for h in range(heads):
            cols = slice(h * HD, (h + 1) * HD)
            q = acc[0, :, cols]
            q_scale = lax.rsqrt(jnp.mean(q * q, axis=-1, keepdims=True) + eps_norm)
            qb[h] = (q * q_scale * qk_gain[0:1, cols]).astype(BF16)
            flash(s, h, t, True)

        @pl.when(s == 0)
        def _():
            wo_copy.wait()

        def gather_sends(c):
            def one(line):
                h_copy(c, line, i, h_part, partner).wait_send()

                @pl.when(jnp.logical_and(has_above, line <= o))
                def _():
                    h_copy(c, line, i, h_up, above).wait_send()

                @pl.when(jnp.logical_and(has_below, line >= o))
                def _():
                    h_copy(c, line, i, h_down, below).wait_send()

            loop(lines, one)

        loop(GATHER_CHUNKS, gather_sends)

        for h in range(heads):
            cols = slice(h * HD, (h + 1) * HD)

            @pl.when(core == 1)
            def _():
                kv_copy(s, t - 1, h, kv_sib.at[h], sibling).wait_recv()
                flash(s, h, t - 1, False)

            def direct(other):
                @pl.when(other < ch)
                def _():
                    g = other * 2 + core
                    got = kv_copy(s, g, h, kv_fwd.at[h, other], sibling)
                    got.wait_recv()
                    got.start()
                    flash(s, h, g, False)

            def passed(other):
                @pl.when(other < ch)
                def _():
                    g = other * 2 + 1 - core
                    kv_copy(s, g, h, kv_fwd.at[h, other], sibling).wait_recv()
                    flash(s, h, g, False)

            loop(chips, direct)
            loop(chips, passed)
            att[:, cols] = (run_acc[h] / run_sum[h]).astype(BF16)

        def partial(c):
            part = pl.ds(pl.multiple_of(c * sw, sw), sw)
            product = jnp.dot(att[...], wo[:, part], preferred_element_type=F32)
            pb[c] = product.astype(BF16).reshape(lines, 2, rows, sw)
            y_copy(c).start()

        loop(SCATTER_CHUNKS, partial)

        def send_up(c):
            for line in range(1, lines):

                @pl.when(line > o)
                def _():
                    u_copy(c, line).start()

        def send_down(c):
            for line in range(lines - 1):

                @pl.when(line < o)
                def _():
                    d_copy(c, line).start()

        def paired(c):
            y_copy(c).wait_recv()
            pb[c, :, i] = (pb[c, :, i].astype(F32) + yb[c].astype(F32)).astype(BF16)

            @pl.when(o == 0)
            def _():
                send_up(c)

            @pl.when(o == lines - 1)
            def _():
                send_down(c)

        def hop(c):
            for line in range(1, lines):

                @pl.when(line > o)
                def _():
                    u_copy(c, line).wait_recv()
                    pb[c, line, i] = (
                        pb[c, line, i].astype(F32) + ub[c, line].astype(F32)
                    ).astype(BF16)
                    u_copy(c, line).start()

        def hop_down(c):
            for line in range(lines - 1):

                @pl.when(line < o)
                def _():
                    d_copy(c, line).wait_recv()
                    pb[c, line, i] = (
                        pb[c, line, i].astype(F32) + db[c, line].astype(F32)
                    ).astype(BF16)
                    d_copy(c, line).start()

        def finish(c):
            part = pl.ds(pl.multiple_of(c * sw, sw), sw)
            out[:, part] += step_size * pb[c, o, i].astype(F32)

            @pl.when(has_below)
            def _():
                u_copy(c, o).wait_recv()
                out[:, part] += step_size * ub[c, o].astype(F32)

            @pl.when(has_above)
            def _():
                d_copy(c, o).wait_recv()
                out[:, part] += step_size * db[c, o].astype(F32)

        def tick(at):
            @pl.when(at < SCATTER_CHUNKS)
            def _():
                paired(at)

            for k in range(1, lines):
                c = at - k
                live = jnp.logical_and(c >= 0, c < SCATTER_CHUNKS)
                if k < lines - 1:

                    @pl.when(jnp.logical_and(live, o == k))
                    def _():
                        hop(c)

                    @pl.when(jnp.logical_and(live, lines - 1 - o == k))
                    def _():
                        hop_down(c)
                else:

                    @pl.when(live)
                    def _():
                        finish(c)

        loop(SCATTER_CHUNKS + lines - 1, tick)

        def scatter_sends(c):
            y_copy(c).wait_send()

            def one(line):
                @pl.when(jnp.logical_and(has_above, line > o))
                def _():
                    u_copy(c, line).wait_send()

                @pl.when(jnp.logical_and(has_below, line < o))
                def _():
                    d_copy(c, line).wait_send()

            loop(lines, one)

        loop(SCATTER_CHUNKS, scatter_sends)
        for h in range(heads):

            @pl.when(core == 0)
            def _():
                kv_copy(s, t, h, kv_sib.at[h], sibling).wait_send()

            def chip_sends(other):
                @pl.when(other > ch)
                def _():
                    kv_copy(s, t, h, kv_chip.at[h, other], other * 2 + core).wait_send()

                @pl.when(other < ch)
                def _():
                    kv_copy(s, other * 2 + core, h, kv_fwd.at[h, other], sibling).wait_send()

            loop(chips, chip_sends)

    loop(STEPS, step)


def shards(states, norm_gain, qkv_weight, qk_gain, out_weight, segment_lengths):
    tm_count, tp_count = lax.axis_size("tm"), lax.axis_size("tp")
    rows, width = states.shape
    head_cols = qkv_weight.shape[2]
    heads = head_cols // HD
    seg = rows * tp_count
    lines, chips = tp_count // 2, tm_count // 2
    gw, sw = width // GATHER_CHUNKS, width // SCATTER_CHUNKS
    position = jnp.arange(seg, dtype=jnp.int32)
    bias = jnp.where(position[None, None, :] < segment_lengths[:, None, None], 0.0, -1e30)
    dma = pltpu.SemaphoreType.DMA
    vmem = pl.BlockSpec(memory_space=pltpu.VMEM)
    hbm = pl.BlockSpec(memory_space=pl.ANY)
    g, s = GATHER_CHUNKS, SCATTER_CHUNKS
    return pl.pallas_call(
        functools.partial(kernel, tm_count, tp_count),
        out_shape=jax.ShapeDtypeStruct((rows, width), F32),
        in_specs=[vmem, vmem, hbm, vmem, hbm, vmem],
        out_specs=vmem,
        scratch_shapes=[
            pltpu.VMEM((3, width, head_cols), BF16),
            pltpu.VMEM((head_cols, width), BF16),
            pltpu.VMEM((g, lines, 2, rows, gw), BF16),
            pltpu.VMEM((3, seg, head_cols), F32),
            pltpu.VMEM((heads, seg, HD), BF16),
            pltpu.VMEM((STEPS, tm_count, heads, 2, seg, HD), BF16),
            pltpu.VMEM((seg, head_cols), BF16),
            pltpu.VMEM((heads, seg, HD), F32),
            pltpu.VMEM((heads, seg, HD), F32),
            pltpu.VMEM((heads, seg, HD), F32),
            pltpu.VMEM((s, lines, 2, rows, sw), BF16),
            pltpu.VMEM((s, lines, rows, sw), BF16),
            pltpu.VMEM((s, lines, rows, sw), BF16),
            pltpu.VMEM((s, lines, rows, sw), BF16),
            dma((g,)),
            dma,
            dma((g, lines, 2)),
            dma((g, lines)),
            dma((g, lines)),
            dma((g, lines)),
            dma((STEPS, tm_count, heads)),
            dma((heads,)),
            dma((heads, chips)),
            dma((heads, chips)),
            dma((s,)),
            dma((s,)),
            dma((s, lines)),
            dma((s, lines)),
            dma((s, lines)),
            dma((s, lines)),
        ],
        compiler_params=pltpu.CompilerParams(
            collective_id=0, has_side_effects=True, vmem_limit_bytes=56 * 1024 * 1024
        ),
        cost_estimate=pl.CostEstimate(
            flops=STEPS * 2 * seg * width * head_cols * 4,
            bytes_accessed=width * head_cols * 8,
            transcendentals=STEPS * heads * seg * seg * tm_count,
        ),
    )(
        states,
        norm_gain.reshape(1, width),
        jnp.transpose(qkv_weight, (1, 0, 2)),
        qk_gain,
        out_weight,
        bias.astype(F32),
    )


def solution(mesh):
    return jax.shard_map(
        shards,
        mesh=mesh,
        in_specs=(
            P(("tm", "tp"), None),
            P(),
            P(None, None, "tp"),
            P(None, "tp"),
            P("tp", None),
            P(),
        ),
        out_specs=P(("tm", "tp"), None),
        check_vma=False,
    )
```

time: 403 us -> 199 us (0.49)
  waiting for transfers between devices: 297 us -> 0 us
  Pallas kernels: 0 us -> 195 us
  matrix products: 38.5 us -> 0 us
  local copies, waits for them, and re-layouts: 35.9 us -> 2.06 us
  between operations: 13.8 us -> 0.01 us
  other arithmetic: 14.7 us -> 1.32 us
    pallas_call x0 -> x1, Pallas kernels: none -> 195 us  [shards(): pl.pallas_call(functools.partial(kernel, tm_count, tp_count), out_shape=j...]
    reduce_scatter x2 -> x0, waiting for transfers between devices: 151 us -> none  [shards(): lax.psum_scatter(jnp.dot(attended, out_weight, preferred_element_type=jnp...]
    all_gather x6 -> x0, waiting for transfers between devices: 146 us -> none  [the longest x2 96.5 us: shards(): lax.all_gather(normed, 'tp', axis=0, tiled=True)]
    dot_general x8 -> x0, matrix products: 38.5 us -> none  [the longest x2 19.8 us: shards(): jnp.dot(lax.all_gather(normed, 'tp', axis=0, tiled=True), wmat, preferred...]
    unnamed x27 -> x1, local copies, waits for them, and re-layouts: 30.8 us -> 2.06 us
    convert_element_type x6 -> x0, other arithmetic: 6.46 us -> none  [the longest x2 3.92 us: shards(): normed = rms_scale(current, norm_gain).astype(jnp.bfloat16)]
    reduce_sum x9 -> x0, other arithmetic: 6.09 us -> none  [the longest x6 3.59 us: rms_scale(): mean_square = jnp.mean(values * values, axis=-1, keepdims=True)]
  transfers between devices with their start and end apart: 8 -> 0, of which waited for: 8 -> 0; matrix products, arithmetic and copies ran while one was open for 9% -> 0% of each run, Pallas kernels for 0% -> 0%
where the time goes in v1:
time: 199 us; the launch traced here: 198 us
  Pallas kernels  195 us (98%)
  local copies, waits for them, and re-layouts  2.06 us (1%)
    pallas_call x1, Pallas kernels, shards(): pl.pallas_call(functools.partial(kernel, tm_count, tp_count), out_shape=j...  195 us

profile of v1, /device:TPU:2, one launch (start us, length us, event | category | flops | bytes accessed | tf_op | source)
XLA Modules:
  0.0 198.5 jit_solution(17512729786193474160)
XLA Ops:
  0.0 1.3 compare_select_fusion.bias
  1.3 195.1 %shard_map.64 = f32[32,6144]{1,0:T(8,128)} custom-call(f32[32,6144]{1,0:T(8,128)} %states.1, f32[1,6144]{1,0:T(1,128)} %bitcast.3, bf16[3,6144,512]{2,1,0:T(8,128)(2,1)} %bitcast.2, f32[2,512]{1,0:T(2,128)} %qk_gain.1, bf16[512,6144]{1,0:T(8,128)(2,1)} %wo_hbm.1, f32[4,1,256]{2,1,0:T(1,128)} %compare_select_fusion.bias), custom_call_target="tpu_custom_call" | custom-call | flops 12884901888 | bytes 25165824 | tf_op jit(solution)/shard_map/pallas_call | solution.py:426
  196.4 2.1 %copy.8 = f32[32,6144]{1,0:T(8,128)} copy(f32[32,6144]{1,0:T(8,128)} %shard_map.64) | data formatting | bytes 1572864

commit v2 on v1

v2 whole, which is shorter than its diff:
```python
import functools
import math

import jax
import jax.numpy as jnp
from jax import lax
from jax.experimental import pallas as pl
from jax.experimental.pallas import tpu as pltpu
from jax.sharding import PartitionSpec as P

HD = 128
STEPS = 2
GATHER_CHUNKS = 6
SCATTER_CHUNKS = 12
LINE_FIRST = 2

eps_norm = 1e-06
step_size = -0.5
BF16 = jnp.bfloat16
F32 = jnp.float32


def remote(src, dst, send_sem, recv_sem, tm, tp):
    return pltpu.make_async_remote_copy(
        src_ref=src,
        dst_ref=dst,
        send_sem=send_sem,
        recv_sem=recv_sem,
        device_id={"tm": tm, "tp": tp},
        device_id_type=pl.DeviceIdType.MESH,
    )


def loop(count, body):
    def step(index, carry):
        body(index)
        return carry

    lax.fori_loop(0, count, step, 0)


def kernel(
    tm_count, tp_count,
    states, gain, w_hbm, qk_gain, wo_hbm, lengths,
    out,
    w, wo, hb, acc, qb, kv, att, run_max, run_acc, pb, yb, ub, db,
    w_sem, wo_sem,
    h_recv, h_part, h_up, h_down,
    kv_recv, kv_sib, kv_chip, kv_fwd,
    y_send, y_recv, u_send, u_recv, d_send, d_recv,
):
    t, p = lax.axis_index("tm"), lax.axis_index("tp")
    lines, chips = tp_count // 2, tm_count // 2
    o, i = p // 2, p % 2
    ch, core = t // 2, t % 2
    partner, above, below = o * 2 + 1 - i, p + 2, p - 2
    sibling = ch * 2 + 1 - core
    has_above, has_below = o < lines - 1, o > 0
    rows, width = states.shape
    seg = rows * tp_count
    head_cols = w.shape[2]
    heads = head_cols // HD
    gw = width // GATHER_CHUNKS
    sw = width // SCATTER_CHUNKS

    def weight_copy(c):
        part = pl.ds(pl.multiple_of(c * gw, gw), gw)
        return pltpu.make_async_copy(w_hbm.at[:, part], w.at[:, part], w_sem.at[c])

    wo_copy = pltpu.make_async_copy(wo_hbm, wo, wo_sem)
    loop(GATHER_CHUNKS, lambda c: weight_copy(c).start())
    wo_copy.start()

    barrier = pltpu.get_barrier_semaphore()

    def greet(tm, tp):
        pl.semaphore_signal(
            barrier, inc=1, device_id={"tm": tm, "tp": tp}, device_id_type=pl.DeviceIdType.MESH
        )

    greet(t, partner)
    greet(sibling, p)

    @pl.when(has_above)
    def _():
        greet(t, above)

    @pl.when(has_below)
    def _():
        greet(t, below)

    for other in range(chips):

        @pl.when(other != ch)
        def _():
            greet(other * 2 + core, p)

    pl.semaphore_wait(
        barrier, 1 + chips + jnp.where(has_above, 1, 0) + jnp.where(has_below, 1, 0)
    )

    out[...] = states[...]

    def h_copy(c, line, side, send_sem, tp):
        ref = hb.at[c, line, side]
        return remote(ref, ref, send_sem.at[c, line, side], h_recv.at[c, line, side], t, tp)

    def h_wait(c, line, side):
        h_copy(c, line, side, h_part, partner).wait_recv()

    def h_both_ways(c, line, side, up, down):
        if up:

            @pl.when(has_above)
            def _():
                h_copy(c, line, side, h_up, above).start()

        if down:

            @pl.when(has_below)
            def _():
                h_copy(c, line, side, h_down, below).start()

    def kv_copy(s, seg_at, h, send_sem, tm):
        ref = kv.at[s, seg_at, h]
        return remote(ref, ref, send_sem, kv_recv.at[s, seg_at, h], tm, p)

    key_at = lax.broadcasted_iota(jnp.int32, (1, seg), 1)
    ones = jnp.ones((seg, HD), BF16)

    def flash(s, h, segments, first):
        scores = [
            lax.dot_general(
                qb[h], kv[s, g, h, 0], (((1,), (1,)), ((), ())), preferred_element_type=F32
            )
            + jnp.where(key_at < lengths[g], 0.0, -1e30)
            for g in segments
        ]
        top = functools.reduce(jnp.maximum, scores)
        top = jnp.max(top, axis=-1, keepdims=True)
        if not first:
            old_top = run_max[h][:, :1]
            top = jnp.maximum(old_top, top)
        update = sum(
            jnp.dot(
                jnp.exp2(part - top).astype(BF16),
                jnp.concatenate([kv[s, g, h, 1], ones], axis=1),
                preferred_element_type=F32,
            )
            for part, g in zip(scores, segments)
        )
        if not first:
            update = update + run_acc[h] * jnp.exp2(old_top - top)
        run_max[h] = jnp.broadcast_to(top, (seg, HD))
        run_acc[h] = update

    def y_copy(c):
        return remote(
            pb.at[c, :, 1 - i], yb.at[c], y_send.at[c], y_recv.at[c], t, partner
        )

    def y_copy_wide(c):
        return remote(
            pb.at[c, o, 1 - i], yb.at[c, 0], y_send.at[c], y_recv.at[c], t, partner
        )

    def rows_of(buffer, c, line, wide):
        return buffer.at[c, line] if wide else buffer.at[c, line, i]

    def u_copy(c, line, wide):
        return remote(
            rows_of(pb, c, line, wide), rows_of(ub, c, line, wide),
            u_send.at[c, line], u_recv.at[c, line], t, above,
        )

    def d_copy(c, line, wide):
        return remote(
            rows_of(pb, c, line, wide), rows_of(db, c, line, wide),
            d_send.at[c, line], d_recv.at[c, line], t, below,
        )

    def step(s):
        square = jnp.zeros((rows, 1), F32)
        for c in range(GATHER_CHUNKS):
            x = out[:, c * gw : (c + 1) * gw]
            square = square + jnp.sum(x * x, axis=-1, keepdims=True)
        scale = lax.rsqrt(square / width + eps_norm)
        last = GATHER_CHUNKS - 1
        for c in [last] + list(range(last)):
            part = slice(c * gw, (c + 1) * gw)
            hb[c, o, i] = (out[:, part] * scale * gain[:, part]).astype(BF16)
            if c < last:
                h_both_ways(c, o, i, True, True)
            h_copy(c, o, i, h_part, partner).start()

        h_both_ways(last, o, i, True, True)
        h_wait(last, o, 1 - i)
        h_both_ways(last, o, 1 - i, True, True)
        for distance in range(1, lines):

            def forward(c):
                @pl.when(o >= distance)
                def _():
                    line = o - distance
                    h_wait(c, line, i)
                    h_both_ways(c, line, i, True, False)
                    h_copy(c, line, i, h_part, partner).start()

                @pl.when(o + distance < lines)
                def _():
                    line = o + distance
                    h_wait(c, line, i)
                    h_both_ways(c, line, i, False, True)
                    h_copy(c, line, i, h_part, partner).start()

            def forward_last():
                for side in (i, 1 - i):

                    @pl.when(o >= distance)
                    def _():
                        h_wait(last, o - distance, side)
                        h_both_ways(last, o - distance, side, True, False)

                    @pl.when(o + distance < lines)
                    def _():
                        h_wait(last, o + distance, side)
                        h_both_ways(last, o + distance, side, False, True)

            loop(last, forward)
            if distance < lines - 1:
                forward_last()

        acc[...] = jnp.zeros_like(acc)

        def project(c):
            @pl.when(c < last)
            def _():
                for line in range(lines):
                    h_wait(c, line, 1 - i)

            @pl.when(c == last)
            def _():
                forward_last()

            @pl.when(s == 0)
            def _():
                weight_copy(c).wait()

            part = pl.ds(pl.multiple_of(c * gw, gw), gw)
            h = hb[c].reshape(seg, gw)
            for j in range(3):
                acc[j] += jnp.dot(h, w[j, part, :], preferred_element_type=F32)

        loop(GATHER_CHUNKS, project)

        for h in range(heads):
            cols = slice(h * HD, (h + 1) * HD)
            k = acc[1, :, cols]
            k_scale = lax.rsqrt(jnp.mean(k * k, axis=-1, keepdims=True) + eps_norm)
            kv[s, t, h, 0] = (k * k_scale * qk_gain[1:2, cols]).astype(BF16)
            kv[s, t, h, 1] = acc[2, :, cols].astype(BF16)
            for other in range(chips):

                @pl.when(other > ch)
                def _():
                    kv_copy(s, t, h, kv_chip.at[h, other], other * 2 + core).start()

            @pl.when(core == 0)
            def _():
                kv_copy(s, t, h, kv_sib.at[h], sibling).start()

        for h in range(heads):
            cols = slice(h * HD, (h + 1) * HD)
            q = acc[0, :, cols]
            q_scale = lax.rsqrt(jnp.mean(q * q, axis=-1, keepdims=True) + eps_norm)
            q_scale = q_scale * (HD ** (-0.5) * math.log2(math.e))
            qb[h] = (q * q_scale * qk_gain[0:1, cols]).astype(BF16)

        @pl.when(core == 0)
        def _():
            for h in range(heads):
                flash(s, h, [t], True)

        @pl.when(core == 1)
        def _():
            for h in range(heads):
                kv_copy(s, t - 1, h, kv_sib.at[h], sibling).wait_recv()
            for h in range(heads):
                flash(s, h, [t, t - 1], True)

        @pl.when(s == 0)
        def _():
            wo_copy.wait()

        def gather_sends(c):
            def one(line):
                h_copy(c, line, i, h_part, partner).wait_send()
                way_sends(c, line, i)

            loop(lines, one)

        def way_sends(c, line, side):
            @pl.when(jnp.logical_and(has_above, line <= o))
            def _():
                h_copy(c, line, side, h_up, above).wait_send()

            @pl.when(jnp.logical_and(has_below, line >= o))
            def _():
                h_copy(c, line, side, h_down, below).wait_send()

        def last_sends(line):
            way_sends(last, line, i)
            way_sends(last, line, 1 - i)

        loop(last, gather_sends)
        h_copy(last, o, i, h_part, partner).wait_send()
        loop(lines, last_sends)

        for group in range(0, heads, 2):
            pair = range(group, min(group + 2, heads))

            def arrived(other):
                @pl.when(other < ch)
                def _():
                    g = other * 2 + core
                    g_passed = other * 2 + 1 - core
                    for h in pair:
                        got = kv_copy(s, g, h, kv_fwd.at[h, other], sibling)
                        got.wait_recv()
                        got.start()
                    for h in pair:
                        kv_copy(s, g_passed, h, kv_fwd.at[h, other], sibling).wait_recv()
                    for h in pair:
                        flash(s, h, [g, g_passed], False)

            loop(chips, arrived)
        for h in range(heads):
            att[:, h * HD : (h + 1) * HD] = (
                run_acc[h][:, :HD] / run_acc[h][:, HD:]
            ).astype(BF16)

        def partial(c):
            part = pl.ds(pl.multiple_of(c * sw, sw), sw)
            product = jnp.dot(att[...], wo[:, part], preferred_element_type=F32)
            pb[c] = product.astype(BF16).reshape(lines, 2, rows, sw)

            @pl.when(c < LINE_FIRST)
            def _():
                start_line(c, True)

            @pl.when(c >= LINE_FIRST)
            def _():
                y_copy(c).start()

        def start_line(c, wide):
            @pl.when(o == 0)
            def _():
                for line in range(1, lines):
                    u_copy(c, line, wide).start()

            @pl.when(o == lines - 1)
            def _():
                for line in range(lines - 1):
                    d_copy(c, line, wide).start()

        loop(SCATTER_CHUNKS, partial)

        def paired(c):
            y_copy(c).wait_recv()
            pb[c, :, i] = (pb[c, :, i].astype(F32) + yb[c].astype(F32)).astype(BF16)
            start_line(c, False)

        def merge(c, line, wide, buffer):
            mine, theirs = rows_of(pb, c, line, wide), rows_of(buffer, c, line, wide)
            mine[...] = (mine[...].astype(F32) + theirs[...].astype(F32)).astype(BF16)

        def hop(c, wide):
            for line in range(1, lines):

                @pl.when(line > o)
                def _():
                    u_copy(c, line, wide).wait_recv()
                    merge(c, line, wide, ub)
                    u_copy(c, line, wide).start()

        def hop_down(c, wide):
            for line in range(lines - 1):

                @pl.when(line < o)
                def _():
                    d_copy(c, line, wide).wait_recv()
                    merge(c, line, wide, db)
                    d_copy(c, line, wide).start()

        def finish(c, wide):
            part = pl.ds(pl.multiple_of(c * sw, sw), sw)

            @pl.when(has_below)
            def _():
                u_copy(c, o, wide).wait_recv()
                merge(c, o, wide, ub)

            @pl.when(has_above)
            def _():
                d_copy(c, o, wide).wait_recv()
                merge(c, o, wide, db)

            if wide:
                y_copy_wide(c).start()
            else:
                out[:, part] += step_size * pb[c, o, i].astype(F32)

        def tick(at):
            @pl.when(jnp.logical_and(at >= LINE_FIRST, at < SCATTER_CHUNKS))
            def _():
                paired(at)

            for k in range(1, lines):
                c = at - k
                for wide, low, high in (
                    (True, 0, LINE_FIRST),
                    (False, LINE_FIRST, SCATTER_CHUNKS),
                ):
                    live = jnp.logical_and(c >= low, c < high)
                    if k < lines - 1:

                        @pl.when(jnp.logical_and(live, o == k))
                        def _():
                            hop(c, wide)

                        @pl.when(jnp.logical_and(live, lines - 1 - o == k))
                        def _():
                            hop_down(c, wide)
                    else:

                        @pl.when(live)
                        def _():
                            finish(c, wide)

        loop(SCATTER_CHUNKS + lines - 1, tick)

        def finish_wide(c):
            part = pl.ds(pl.multiple_of(c * sw, sw), sw)
            y_copy_wide(c).wait_recv()
            out[:, part] += step_size * (pb[c, o, i].astype(F32) + yb[c, 0].astype(F32))

        loop(LINE_FIRST, finish_wide)

        def scatter_sends(c):
            for wide in (True, False):

                @pl.when((c < LINE_FIRST) == wide)
                def _():
                    (y_copy_wide if wide else y_copy)(c).wait_send()

                    def one(line):
                        @pl.when(jnp.logical_and(has_above, line > o))
                        def _():
                            u_copy(c, line, wide).wait_send()

                        @pl.when(jnp.logical_and(has_below, line < o))
                        def _():
                            d_copy(c, line, wide).wait_send()

                    loop(lines, one)

        loop(SCATTER_CHUNKS, scatter_sends)
        for h in range(heads):

            @pl.when(core == 0)
            def _():
                kv_copy(s, t, h, kv_sib.at[h], sibling).wait_send()

            def chip_sends(other):
                @pl.when(other > ch)
                def _():
                    kv_copy(s, t, h, kv_chip.at[h, other], other * 2 + core).wait_send()

                @pl.when(other < ch)
                def _():
                    kv_copy(s, other * 2 + core, h, kv_fwd.at[h, other], sibling).wait_send()

            loop(chips, chip_sends)

    loop(STEPS, step)


def shards(states, norm_gain, qkv_weight, qk_gain, out_weight, segment_lengths):
    tm_count, tp_count = lax.axis_size("tm"), lax.axis_size("tp")
    rows, width = states.shape
    head_cols = qkv_weight.shape[2]
    heads = head_cols // HD
    seg = rows * tp_count
    lines, chips = tp_count // 2, tm_count // 2
    gw, sw = width // GATHER_CHUNKS, width // SCATTER_CHUNKS
    dma = pltpu.SemaphoreType.DMA
    vmem = pl.BlockSpec(memory_space=pltpu.VMEM)
    smem = pl.BlockSpec(memory_space=pltpu.SMEM)
    hbm = pl.BlockSpec(memory_space=pl.ANY)
    g, s = GATHER_CHUNKS, SCATTER_CHUNKS
    return pl.pallas_call(
        functools.partial(kernel, tm_count, tp_count),
        out_shape=jax.ShapeDtypeStruct((rows, width), F32),
        in_specs=[vmem, vmem, hbm, vmem, hbm, smem],
        out_specs=vmem,
        scratch_shapes=[
            pltpu.VMEM((3, width, head_cols), BF16),
            pltpu.VMEM((head_cols, width), BF16),
            pltpu.VMEM((g, lines, 2, rows, gw), BF16),
            pltpu.VMEM((3, seg, head_cols), F32),
            pltpu.VMEM((heads, seg, HD), BF16),
            pltpu.VMEM((STEPS, tm_count, heads, 2, seg, HD), BF16),
            pltpu.VMEM((seg, head_cols), BF16),
            pltpu.VMEM((heads, seg, HD), F32),
            pltpu.VMEM((heads, seg, 2 * HD), F32),
            pltpu.VMEM((s, lines, 2, rows, sw), BF16),
            pltpu.VMEM((s, lines, rows, sw), BF16),
            pltpu.VMEM((s, lines, 2, rows, sw), BF16),
            pltpu.VMEM((s, lines, 2, rows, sw), BF16),
            dma((g,)),
            dma,
            dma((g, lines, 2)),
            dma((g, lines, 2)),
            dma((g, lines, 2)),
            dma((g, lines, 2)),
            dma((STEPS, tm_count, heads)),
            dma((heads,)),
            dma((heads, chips)),
            dma((heads, chips)),
            dma((s,)),
            dma((s,)),
            dma((s, lines)),
            dma((s, lines)),
            dma((s, lines)),
            dma((s, lines)),
        ],
        compiler_params=pltpu.CompilerParams(
            collective_id=0, has_side_effects=True, vmem_limit_bytes=56 * 1024 * 1024
        ),
        cost_estimate=pl.CostEstimate(
            flops=STEPS * 2 * seg * width * head_cols * 4,
            bytes_accessed=width * head_cols * 8,
            transcendentals=STEPS * heads * seg * seg * tm_count,
        ),
    )(
        states,
        norm_gain.reshape(1, width),
        jnp.transpose(qkv_weight, (1, 0, 2)),
        qk_gain,
        out_weight,
        segment_lengths,
    )


def solution(mesh):
    return jax.shard_map(
        shards,
        mesh=mesh,
        in_specs=(
            P(("tm", "tp"), None),
            P(),
            P(None, None, "tp"),
            P(None, "tp"),
            P("tp", None),
            P(),
        ),
        out_specs=P(("tm", "tp"), None),
        check_vma=False,
    )
```

time: 199 us -> 181 us (0.910)
  Pallas kernels: 195 us -> 179 us
    pallas_call x1, Pallas kernels: 195 us -> 179 us  [shards(): pl.pallas_call(functools.partial(kernel, tm_count, tp_count), out_shape=j...]
where the time goes in v2:
time: 181 us
  Pallas kernels  179 us (99%)
  local copies, waits for them, and re-layouts  2.06 us (1%)
    pallas_call x1, Pallas kernels, shards(): pl.pallas_call(functools.partial(kernel, tm_count, tp_count), out_shape=j...  179 us

profile of v2, /device:TPU:2, one launch (start us, length us, event | category | flops | bytes accessed | tf_op | source)
XLA Modules:
  0.0 180.9 jit_solution(12308384468945150725)
XLA Ops:
  0.0 178.9 %shard_map.64 = f32[32,6144]{1,0:T(8,128)} custom-call(f32[32,6144]{1,0:T(8,128)} %states.1, f32[1,6144]{1,0:T(1,128)} %bitcast.3, bf16[3,6144,512]{2,1,0:T(8,128)(2,1)} %bitcast.2, f32[2,512]{1,0:T(2,128)} %qk_gain.1, bf16[512,6144]{1,0:T(8,128)(2,1)} %wo_hbm.1, s32[4]{0:T(128)} %lengths.1), custom_call_target="tpu_custom_call" | custom-call | flops 12884901888 | bytes 25165824 | tf_op jit(solution)/shard_map/pallas_call | solution.py:501
  178.9 2.1 %copy.8 = f32[32,6144]{1,0:T(8,128)} copy(f32[32,6144]{1,0:T(8,128)} %shard_map.64) | data formatting | bytes 1572864

commit v3 on v2

--- a/solution.py
+++ b/solution.py
@@ -43,9 +43,10 @@
     tm_count, tp_count,
     states, gain, w_hbm, qk_gain, wo_hbm, lengths,
     out,
-    w, wo, hb, acc, qb, kv, att, run_max, run_acc, pb, yb, ub, db,
+    w, wo, hb, rb, acc, qb, kv, att, run_max, run_acc, pb, yb, ub, db,
     w_sem, wo_sem,
     h_recv, h_part, h_up, h_down,
+    r_recv, r_part, r_up, r_down,
     kv_recv, kv_sib, kv_chip, kv_fwd,
     y_send, y_recv, u_send, u_recv, d_send, d_recv,
 ):
@@ -62,6 +63,8 @@
     heads = head_cols // HD
     gw = width // GATHER_CHUNKS
     sw = width // SCATTER_CHUNKS
+    per_gather = SCATTER_CHUNKS // GATHER_CHUNKS
+    both = 0
 
     def weight_copy(c):
         part = pl.ds(pl.multiple_of(c * gw, gw), gw)
@@ -95,11 +98,36 @@
         def _():
             greet(other * 2 + core, p)
 
+    out[...] = states[...]
+
+    def prepare(c):
+        part = pl.ds(pl.multiple_of(c * gw, gw), gw)
+        hb[c, o, i] = (out[:, part] * gain[:, part]).astype(BF16)
+
+    on_diagonal = lax.broadcasted_iota(
+        jnp.int32, (rows, HD), 0
+    ) == lax.broadcasted_iota(jnp.int32, (rows, HD), 1)
+
+    def prepare_scale():
+        square = jnp.zeros((rows, 1), F32)
+        for c in range(GATHER_CHUNKS):
+            x = out[:, c * gw : (c + 1) * gw]
+            square = square + jnp.sum(x * x, axis=-1, keepdims=True)
+        scale = lax.rsqrt(square / width + eps_norm)
+        laid = jnp.sum(jnp.where(on_diagonal, scale, 0.0), axis=0, keepdims=True)
+        rb[o, i] = jnp.broadcast_to(laid, (8, HD))
+
+    def scale_column(line, side):
+        laid = jnp.broadcast_to(rb[line, side][0:1], (rows, HD))
+        return jnp.sum(jnp.where(on_diagonal, laid, 0.0), axis=-1, keepdims=True)
+
+    loop(GATHER_CHUNKS, prepare)
+    prepare_scale()
+
     pl.semaphore_wait(
         barrier, 1 + chips + jnp.where(has_above, 1, 0) + jnp.where(has_below, 1, 0)
     )
 
-    out[...] = states[...]
 
     def h_copy(c, line, side, send_sem, tp):
         ref = hb.at[c, line, side]
@@ -120,6 +148,29 @@
             @pl.when(has_below)
             def _():
                 h_copy(c, line, side, h_down, below).start()
+
+    def r_copy(line, side, send_sem, tp):
+        ref = rb.at[line, side]
+        return remote(ref, ref, send_sem.at[line], r_recv.at[line, side], t, tp)
+
+    def r_forward(line, up, down):
+        if up:
+
+            @pl.when(has_above)
+            def _():
+                r_copy(line, i, r_up, above).start()
+
+        if down:
+
+            @pl.when(has_below)
+            def _():
+                r_copy(line, i, r_down, below).start()
+
+        r_copy(line, i, r_part, partner).start()
+
+    def send_own(c):
+        h_both_ways(c, o, i, True, True)
+        h_copy(c, o, i, h_part, partner).start()
 
     def kv_copy(s, seg_at, h, send_sem, tm):
         ref = kv.at[s, seg_at, h]
@@ -180,22 +231,10 @@
         )
 
     def step(s):
-        square = jnp.zeros((rows, 1), F32)
-        for c in range(GATHER_CHUNKS):
-            x = out[:, c * gw : (c + 1) * gw]
-            square = square + jnp.sum(x * x, axis=-1, keepdims=True)
-        scale = lax.rsqrt(square / width + eps_norm)
-        last = GATHER_CHUNKS - 1
-        for c in [last] + list(range(last)):
-            part = slice(c * gw, (c + 1) * gw)
-            hb[c, o, i] = (out[:, part] * scale * gain[:, part]).astype(BF16)
-            if c < last:
-                h_both_ways(c, o, i, True, True)
-            h_copy(c, o, i, h_part, partner).start()
-
-        h_both_ways(last, o, i, True, True)
-        h_wait(last, o, 1 - i)
-        h_both_ways(last, o, 1 - i, True, True)
+        h_both_ways(both, o, i, True, True)
+        h_wait(both, o, 1 - i)
+        h_both_ways(both, o, 1 - i, True, True)
+        acc[...] = jnp.zeros_like(acc)
         for distance in range(1, lines):
 
             def forward(c):
@@ -213,34 +252,45 @@
                     h_both_ways(c, line, i, False, True)
                     h_copy(c, line, i, h_part, partner).start()
 
-            def forward_last():
+            def forward_both():
                 for side in (i, 1 - i):
 
                     @pl.when(o >= distance)
                     def _():
-                        h_wait(last, o - distance, side)
-                        h_both_ways(last, o - distance, side, True, False)
+                        h_wait(both, o - distance, side)
+                        h_both_ways(both, o - distance, side, True, False)
 
                     @pl.when(o + distance < lines)
                     def _():
-                        h_wait(last, o + distance, side)
-                        h_both_ways(last, o + distance, side, False, True)
-
-            loop(last, forward)
+                        h_wait(both, o + distance, side)
+                        h_both_ways(both, o + distance, side, False, True)
+
+            def forward_scale():
+                @pl.when(o >= distance)
+                def _():
+                    r_copy(o - distance, i, r_part, partner).wait_recv()
+                    r_forward(o - distance, True, False)
+
+                @pl.when(o + distance < lines)
+                def _():
+                    r_copy(o + distance, i, r_part, partner).wait_recv()
+                    r_forward(o + distance, False, True)
+
             if distance < lines - 1:
-                forward_last()
-
-        acc[...] = jnp.zeros_like(acc)
+                loop(GATHER_CHUNKS - 1, lambda c: forward(c + 1))
+                forward_scale()
+                forward_both()
 
         def project(c):
-            @pl.when(c < last)
+            @pl.when(c != both)
             def _():
                 for line in range(lines):
                     h_wait(c, line, 1 - i)
 
-            @pl.when(c == last)
-            def _():
-                forward_last()
+            @pl.when(c == both)
+            def _():
+                forward_scale()
+                forward_both()
 
             @pl.when(s == 0)
             def _():
@@ -251,7 +301,22 @@
             for j in range(3):
                 acc[j] += jnp.dot(h, w[j, part, :], preferred_element_type=F32)
 
-        loop(GATHER_CHUNKS, project)
+        def farthest(at):
+            @pl.when(at < GATHER_CHUNKS - 1)
+            def _():
+                forward(at + 1)
+
+            @pl.when(at >= 2)
+            def _():
+                project(jnp.where(at == GATHER_CHUNKS + 1, both, at - 1))
+
+        loop(GATHER_CHUNKS + 2, farthest)
+        for line in range(lines):
+            r_copy(line, 1 - i, r_part, partner).wait_recv()
+        for line in range(lines):
+            for side in range(2):
+                here = pl.ds((line * 2 + side) * rows, rows)
+                acc[:, here, :] = acc[:, here, :] * scale_column(line, side)
 
         for h in range(heads):
             cols = slice(h * HD, (h + 1) * HD)
@@ -299,6 +364,17 @@
 
             loop(lines, one)
 
+        def scale_sends(line):
+            r_copy(line, i, r_part, partner).wait_send()
+
+            @pl.when(jnp.logical_and(has_above, line <= o))
+            def _():
+                r_copy(line, i, r_up, above).wait_send()
+
+            @pl.when(jnp.logical_and(has_below, line >= o))
+            def _():
+                r_copy(line, i, r_down, below).wait_send()
+
         def way_sends(c, line, side):
             @pl.when(jnp.logical_and(has_above, line <= o))
             def _():
@@ -308,13 +384,14 @@
             def _():
                 h_copy(c, line, side, h_down, below).wait_send()
 
-        def last_sends(line):
-            way_sends(last, line, i)
-            way_sends(last, line, 1 - i)
-
-        loop(last, gather_sends)
-        h_copy(last, o, i, h_part, partner).wait_send()
-        loop(lines, last_sends)
+        def both_sends(line):
+            way_sends(both, line, i)
+            way_sends(both, line, 1 - i)
+
+        loop(GATHER_CHUNKS - 1, lambda c: gather_sends(c + 1))
+        h_copy(both, o, i, h_part, partner).wait_send()
+        loop(lines, both_sends)
+        loop(lines, scale_sends)
 
         for group in range(0, heads, 2):
             pair = range(group, min(group + 2, heads))
@@ -355,7 +432,7 @@
         def start_line(c, wide):
             @pl.when(o == 0)
             def _():
-                for line in range(1, lines):
+                for line in range(lines - 1, 0, -1):
                     u_copy(c, line, wide).start()
 
             @pl.when(o == lines - 1)
@@ -375,7 +452,7 @@
             mine[...] = (mine[...].astype(F32) + theirs[...].astype(F32)).astype(BF16)
 
         def hop(c, wide):
-            for line in range(1, lines):
+            for line in range(lines - 1, 0, -1):
 
                 @pl.when(line > o)
                 def _():
@@ -409,6 +486,11 @@
                 y_copy_wide(c).start()
             else:
                 out[:, part] += step_size * pb[c, o, i].astype(F32)
+
+                @pl.when(jnp.logical_and(s < STEPS - 1, c % per_gather == per_gather - 1))
+                def _():
+                    prepare(c // per_gather)
+                    send_own(c // per_gather)
 
         def tick(at):
             @pl.when(jnp.logical_and(at >= LINE_FIRST, at < SCATTER_CHUNKS))
@@ -437,14 +519,29 @@
                         def _():
                             finish(c, wide)
 
-        loop(SCATTER_CHUNKS + lines - 1, tick)
-
         def finish_wide(c):
             part = pl.ds(pl.multiple_of(c * sw, sw), sw)
             y_copy_wide(c).wait_recv()
             out[:, part] += step_size * (pb[c, o, i].astype(F32) + yb[c, 0].astype(F32))
 
-        loop(LINE_FIRST, finish_wide)
+        def tick_all(at):
+            tick(at)
+
+            @pl.when(at == SCATTER_CHUNKS)
+            def _():
+                loop(LINE_FIRST, finish_wide)
+
+                @pl.when(s < STEPS - 1)
+                def _():
+                    prepare(both)
+                    h_copy(both, o, i, h_part, partner).start()
+
+        loop(SCATTER_CHUNKS + lines - 1, tick_all)
+
+        @pl.when(s < STEPS - 1)
+        def _():
+            prepare_scale()
+            r_forward(o, True, True)
 
         def scatter_sends(c):
             for wide in (True, False):
@@ -482,6 +579,10 @@
 
             loop(chips, chip_sends)
 
+    h_copy(both, o, i, h_part, partner).start()
+    for c in range(1, GATHER_CHUNKS):
+        send_own(c)
+    r_forward(o, True, True)
     loop(STEPS, step)
 
 
@@ -507,6 +608,7 @@
             pltpu.VMEM((3, width, head_cols), BF16),
             pltpu.VMEM((head_cols, width), BF16),
             pltpu.VMEM((g, lines, 2, rows, gw), BF16),
+            pltpu.VMEM((lines, 2, 8, HD), F32),
             pltpu.VMEM((3, seg, head_cols), F32),
             pltpu.VMEM((heads, seg, HD), BF16),
             pltpu.VMEM((STEPS, tm_count, heads, 2, seg, HD), BF16),
@@ -523,6 +625,10 @@
             dma((g, lines, 2)),
             dma((g, lines, 2)),
             dma((g, lines, 2)),
+            dma((lines, 2)),
+            dma((lines,)),
+            dma((lines,)),
+            dma((lines,)),
             dma((STEPS, tm_count, heads)),
             dma((heads,)),
             dma((heads, chips)),

time: 181 us -> 178 us (0.983)
  Pallas kernels: 179 us -> 175 us
    pallas_call x1, Pallas kernels: 179 us -> 175 us  [shards(): pl.pallas_call(functools.partial(kernel, tm_count, tp_count), out_shape=j...]
where the time goes in v3:
time: 178 us; the launch traced here: 177 us
  Pallas kernels  175 us (98%)
  local copies, waits for them, and re-layouts  2.06 us (1%)
    pallas_call x1, Pallas kernels, shards(): pl.pallas_call(functools.partial(kernel, tm_count, tp_count), out_shape=j...  175 us

profile of v3, /device:TPU:2, one launch (start us, length us, event | category | flops | bytes accessed | tf_op | source)
XLA Modules:
  0.0 177.2 jit_solution(13208811151253711753)
XLA Ops:
  0.0 175.2 %shard_map.64 = f32[32,6144]{1,0:T(8,128)} custom-call(f32[32,6144]{1,0:T(8,128)} %states.1, f32[1,6144]{1,0:T(1,128)} %bitcast.3, bf16[3,6144,512]{2,1,0:T(8,128)(2,1)} %bitcast.2, f32[2,512]{1,0:T(2,128)} %qk_gain.1, bf16[512,6144]{1,0:T(8,128)(2,1)} %wo_hbm.1, s32[4]{0:T(128)} %lengths.1), custom_call_target="tpu_custom_call" | custom-call | flops 12884901888 | bytes 25165824 | tf_op jit(solution)/shard_map/pallas_call | solution.py:602
  175.2 2.1 %copy.8 = f32[32,6144]{1,0:T(8,128)} copy(f32[32,6144]{1,0:T(8,128)} %shard_map.64) | data formatting | bytes 1572864

commit v4 on v3

--- a/solution.py
+++ b/solution.py
@@ -11,6 +11,7 @@
 HD = 128
 STEPS = 2
 GATHER_CHUNKS = 6
+GROUP = 3
 SCATTER_CHUNKS = 12
 LINE_FIRST = 2
 
@@ -29,6 +30,10 @@
         device_id={"tm": tm, "tp": tp},
         device_id_type=pl.DeviceIdType.MESH,
     )
+
+
+def halves_of(rows):
+    return 2 if rows % 32 == 0 else 1
 
 
 def loop(count, body):
@@ -61,17 +66,20 @@
     seg = rows * tp_count
     head_cols = w.shape[2]
     heads = head_cols // HD
-    gw = width // GATHER_CHUNKS
+    halves = halves_of(rows)
+    rh, sh = rows // halves, seg // halves
+    gw = width * halves // GATHER_CHUNKS
     sw = width // SCATTER_CHUNKS
-    per_gather = SCATTER_CHUNKS // GATHER_CHUNKS
-    both = 0
+    parts = width // gw
+    per_gather = gw // sw
+    both = GROUP
 
     def weight_copy(c):
         part = pl.ds(pl.multiple_of(c * gw, gw), gw)
         return pltpu.make_async_copy(w_hbm.at[:, part], w.at[:, part], w_sem.at[c])
 
     wo_copy = pltpu.make_async_copy(wo_hbm, wo, wo_sem)
-    loop(GATHER_CHUNKS, lambda c: weight_copy(c).start())
+    loop(parts, lambda c: weight_copy(c).start())
     wo_copy.start()
 
     barrier = pltpu.get_barrier_semaphore()
@@ -101,8 +109,9 @@
     out[...] = states[...]
 
     def prepare(c):
-        part = pl.ds(pl.multiple_of(c * gw, gw), gw)
-        hb[c, o, i] = (out[:, part] * gain[:, part]).astype(BF16)
+        part = pl.ds(pl.multiple_of(c % parts * gw, gw), gw)
+        here = pl.ds(pl.multiple_of(c // parts * rh, rh), rh)
+        hb[c, o, i] = (out[here, part] * gain[:, part]).astype(BF16)
 
     on_diagonal = lax.broadcasted_iota(
         jnp.int32, (rows, HD), 0
@@ -110,8 +119,8 @@
 
     def prepare_scale():
         square = jnp.zeros((rows, 1), F32)
-        for c in range(GATHER_CHUNKS):
-            x = out[:, c * gw : (c + 1) * gw]
+        for c in range(SCATTER_CHUNKS):
+            x = out[:, c * sw : (c + 1) * sw]
             square = square + jnp.sum(x * x, axis=-1, keepdims=True)
         scale = lax.rsqrt(square / width + eps_norm)
         laid = jnp.sum(jnp.where(on_diagonal, scale, 0.0), axis=0, keepdims=True)
@@ -172,17 +181,18 @@
         h_both_ways(c, o, i, True, True)
         h_copy(c, o, i, h_part, partner).start()
 
-    def kv_copy(s, seg_at, h, send_sem, tm):
-        ref = kv.at[s, seg_at, h]
-        return remote(ref, ref, send_sem, kv_recv.at[s, seg_at, h], tm, p)
+    def kv_copy(s, seg_at, h, half, send_sem, tm):
+        ref = kv.at[s, seg_at, h, half]
+        return remote(ref, ref, send_sem.at[half], kv_recv.at[s, seg_at, h, half], tm, p)
 
     key_at = lax.broadcasted_iota(jnp.int32, (1, seg), 1)
+    key_at = key_at % sh // rh * rows + key_at // sh * rh + key_at % rh
     ones = jnp.ones((seg, HD), BF16)
 
     def flash(s, h, segments, first):
         scores = [
             lax.dot_general(
-                qb[h], kv[s, g, h, 0], (((1,), (1,)), ((), ())), preferred_element_type=F32
+                qb[h], kv[s, g, h, :, 0].reshape(seg, HD), (((1,), (1,)), ((), ())), preferred_element_type=F32
             )
             + jnp.where(key_at < lengths[g], 0.0, -1e30)
             for g in segments
@@ -195,7 +205,7 @@
         update = sum(
             jnp.dot(
                 jnp.exp2(part - top).astype(BF16),
-                jnp.concatenate([kv[s, g, h, 1], ones], axis=1),
+                jnp.concatenate([kv[s, g, h, :, 1].reshape(seg, HD), ones], axis=1),
                 preferred_element_type=F32,
             )
             for part, g in zip(scores, segments)
@@ -231,115 +241,144 @@
         )
 
     def step(s):
+        def forward(c, distance):
+            @pl.when(o >= distance)
+            def _():
+                line = o - distance
+                h_wait(c, line, i)
+                h_both_ways(c, line, i, True, False)
+                h_copy(c, line, i, h_part, partner).start()
+
+            @pl.when(o + distance < lines)
+            def _():
+                line = o + distance
+                h_wait(c, line, i)
+                h_both_ways(c, line, i, False, True)
+                h_copy(c, line, i, h_part, partner).start()
+
+        def forward_both(distance):
+            for side in (i, 1 - i):
+
+                @pl.when(o >= distance)
+                def _():
+                    h_wait(both, o - distance, side)
+                    h_both_ways(both, o - distance, side, True, False)
+
+                @pl.when(o + distance < lines)
+                def _():
+                    h_wait(both, o + distance, side)
+                    h_both_ways(both, o + distance, side, False, True)
+
+        def forward_scale(distance):
+            @pl.when(o >= distance)
+            def _():
+                r_copy(o - distance, i, r_part, partner).wait_recv()
+                r_forward(o - distance, True, False)
+
+            @pl.when(o + distance < lines)
+            def _():
+                r_copy(o + distance, i, r_part, partner).wait_recv()
+                r_forward(o + distance, False, True)
+
+        def project(c):
+            @pl.when(c != both)
+            def _():
+                for line in range(lines):
+                    h_wait(c, line, 1 - i)
+
+            @pl.when(jnp.logical_and(s == 0, c < parts))
+            def _():
+                weight_copy(c).wait()
+
+            part = pl.ds(pl.multiple_of(c % parts * gw, gw), gw)
+            h = hb[c].reshape(sh, gw)
+            for j in range(3):
+                acc[c // parts, j] += jnp.dot(h, w[j, part, :], preferred_element_type=F32)
+
+        def scales(half):
+            return jnp.concatenate(
+                [
+                    scale_column(line, side)[half * rh : (half + 1) * rh]
+                    for line in range(lines)
+                    for side in range(2)
+                ],
+                axis=0,
+            )
+
+        def emit_keys(half):
+            scale = scales(half)
+            for h in range(heads):
+                cols = slice(h * HD, (h + 1) * HD)
+                k = acc[half, 1, :, cols] * scale
+                k_scale = lax.rsqrt(jnp.mean(k * k, axis=-1, keepdims=True) + eps_norm)
+                kv[s, t, h, half, 0] = (k * k_scale * qk_gain[1:2, cols]).astype(BF16)
+                kv[s, t, h, half, 1] = (acc[half, 2, :, cols] * scale).astype(BF16)
+                for other in range(chips):
+
+                    @pl.when(other > ch)
+                    def _():
+                        kv_copy(
+                            s, t, h, half, kv_chip.at[h, other], other * 2 + core
+                        ).start()
+
+                @pl.when(core == 0)
+                def _():
+                    kv_copy(s, t, h, half, kv_sib.at[h], sibling).start()
+
+        def emit_queries(half):
+            scale = scales(half)
+            for h in range(heads):
+                cols = slice(h * HD, (h + 1) * HD)
+                q = acc[half, 0, :, cols] * scale
+                q_scale = lax.rsqrt(jnp.mean(q * q, axis=-1, keepdims=True) + eps_norm)
+                q_scale = q_scale * (HD ** (-0.5) * math.log2(math.e))
+                qb[h, half * sh : (half + 1) * sh] = (
+                    q * q_scale * qk_gain[0:1, cols]
+                ).astype(BF16)
+
+        rest = GATHER_CHUNKS - GROUP - 1
+        acc[...] = jnp.zeros_like(acc)
+        for distance in range(1, lines - 1):
+            loop(GROUP, lambda c: forward(c, distance))
+            forward_scale(distance)
+        loop(rest, lambda c: h_both_ways(c + both + 1, o, i, True, True))
         h_both_ways(both, o, i, True, True)
         h_wait(both, o, 1 - i)
         h_both_ways(both, o, 1 - i, True, True)
-        acc[...] = jnp.zeros_like(acc)
-        for distance in range(1, lines):
-
-            def forward(c):
-                @pl.when(o >= distance)
-                def _():
-                    line = o - distance
-                    h_wait(c, line, i)
-                    h_both_ways(c, line, i, True, False)
-                    h_copy(c, line, i, h_part, partner).start()
-
-                @pl.when(o + distance < lines)
-                def _():
-                    line = o + distance
-                    h_wait(c, line, i)
-                    h_both_ways(c, line, i, False, True)
-                    h_copy(c, line, i, h_part, partner).start()
-
-            def forward_both():
-                for side in (i, 1 - i):
-
-                    @pl.when(o >= distance)
-                    def _():
-                        h_wait(both, o - distance, side)
-                        h_both_ways(both, o - distance, side, True, False)
-
-                    @pl.when(o + distance < lines)
-                    def _():
-                        h_wait(both, o + distance, side)
-                        h_both_ways(both, o + distance, side, False, True)
-
-            def forward_scale():
-                @pl.when(o >= distance)
-                def _():
-                    r_copy(o - distance, i, r_part, partner).wait_recv()
-                    r_forward(o - distance, True, False)
-
-                @pl.when(o + distance < lines)
-                def _():
-                    r_copy(o + distance, i, r_part, partner).wait_recv()
-                    r_forward(o + distance, False, True)
-
-            if distance < lines - 1:
-                loop(GATHER_CHUNKS - 1, lambda c: forward(c + 1))
-                forward_scale()
-                forward_both()
-
-        def project(c):
-            @pl.when(c != both)
-            def _():
-                for line in range(lines):
-                    h_wait(c, line, 1 - i)
-
-            @pl.when(c == both)
-            def _():
-                forward_scale()
-                forward_both()
-
-            @pl.when(s == 0)
-            def _():
-                weight_copy(c).wait()
-
-            part = pl.ds(pl.multiple_of(c * gw, gw), gw)
-            h = hb[c].reshape(seg, gw)
-            for j in range(3):
-                acc[j] += jnp.dot(h, w[j, part, :], preferred_element_type=F32)
-
-        def farthest(at):
-            @pl.when(at < GATHER_CHUNKS - 1)
-            def _():
-                forward(at + 1)
-
-            @pl.when(at >= 2)
-            def _():
-                project(jnp.where(at == GATHER_CHUNKS + 1, both, at - 1))
-
-        loop(GATHER_CHUNKS + 2, farthest)
+        loop(GROUP, lambda c: forward(c, lines - 1))
+        forward_scale(lines - 1)
+        loop(rest, lambda c: h_copy(c + both + 1, o, i, h_part, partner).start())
         for line in range(lines):
             r_copy(line, 1 - i, r_part, partner).wait_recv()
-        for line in range(lines):
-            for side in range(2):
-                here = pl.ds((line * 2 + side) * rows, rows)
-                acc[:, here, :] = acc[:, here, :] * scale_column(line, side)
-
-        for h in range(heads):
-            cols = slice(h * HD, (h + 1) * HD)
-            k = acc[1, :, cols]
-            k_scale = lax.rsqrt(jnp.mean(k * k, axis=-1, keepdims=True) + eps_norm)
-            kv[s, t, h, 0] = (k * k_scale * qk_gain[1:2, cols]).astype(BF16)
-            kv[s, t, h, 1] = acc[2, :, cols].astype(BF16)
-            for other in range(chips):
-
-                @pl.when(other > ch)
-                def _():
-                    kv_copy(s, t, h, kv_chip.at[h, other], other * 2 + core).start()
-
-            @pl.when(core == 0)
-            def _():
-                kv_copy(s, t, h, kv_sib.at[h], sibling).start()
-
-        for h in range(heads):
-            cols = slice(h * HD, (h + 1) * HD)
-            q = acc[0, :, cols]
-            q_scale = lax.rsqrt(jnp.mean(q * q, axis=-1, keepdims=True) + eps_norm)
-            q_scale = q_scale * (HD ** (-0.5) * math.log2(math.e))
-            qb[h] = (q * q_scale * qk_gain[0:1, cols]).astype(BF16)
+
+        for distance in range(1, lines - 1):
+
+            def second(c):
+                forward(c + both + 1, distance)
+                if distance == 1:
+                    project(c)
+
+            loop(rest, second)
+            forward_both(distance)
+            if distance == 1:
+                loop(GROUP - rest, lambda c: project(c + rest))
+                if halves == 2:
+                    emit_keys(0)
+            elif distance == 2 and halves == 2:
+                emit_queries(0)
+
+        loop(rest, lambda c: forward(c + both + 1, lines - 1))
+
+        def final(c):
+            @pl.when(c == rest)
+            def _():
+                forward_both(lines - 1)
+
+            project(jnp.where(c == rest, both, c + both + 1))
+
+        loop(rest + 1, final)
+        emit_keys(halves - 1)
+        emit_queries(halves - 1)
 
         @pl.when(core == 0)
         def _():
@@ -349,7 +388,8 @@
         @pl.when(core == 1)
         def _():
             for h in range(heads):
-                kv_copy(s, t - 1, h, kv_sib.at[h], sibling).wait_recv()
+                for half in range(halves):
+                    kv_copy(s, t - 1, h, half, kv_sib.at[h], sibling).wait_recv()
             for h in range(heads):
                 flash(s, h, [t, t - 1], True)
 
@@ -388,7 +428,12 @@
             way_sends(both, line, i)
             way_sends(both, line, 1 - i)
 
-        loop(GATHER_CHUNKS - 1, lambda c: gather_sends(c + 1))
+        def chunk_sends(c):
+            @pl.when(c != both)
+            def _():
+                gather_sends(c)
+
+        loop(GATHER_CHUNKS, chunk_sends)
         h_copy(both, o, i, h_part, partner).wait_send()
         loop(lines, both_sends)
         loop(lines, scale_sends)
@@ -402,11 +447,15 @@
                     g = other * 2 + core
                     g_passed = other * 2 + 1 - core
                     for h in pair:
-                        got = kv_copy(s, g, h, kv_fwd.at[h, other], sibling)
-                        got.wait_recv()
-                        got.start()
+                        for half in range(halves):
+                            got = kv_copy(s, g, h, half, kv_fwd.at[h, other], sibling)
+                            got.wait_recv()
+                            got.start()
                     for h in pair:
-                        kv_copy(s, g_passed, h, kv_fwd.at[h, other], sibling).wait_recv()
+                        for half in range(halves):
+                            kv_copy(
+                                s, g_passed, h, half, kv_fwd.at[h, other], sibling
+                            ).wait_recv()
                     for h in pair:
                         flash(s, h, [g, g_passed], False)
 
@@ -419,7 +468,12 @@
         def partial(c):
             part = pl.ds(pl.multiple_of(c * sw, sw), sw)
             product = jnp.dot(att[...], wo[:, part], preferred_element_type=F32)
-            pb[c] = product.astype(BF16).reshape(lines, 2, rows, sw)
+            for half in range(halves):
+                pb[c, :, :, half * rh : (half + 1) * rh] = (
+                    product[half * sh : (half + 1) * sh]
+                    .astype(BF16)
+                    .reshape(lines, 2, rh, sw)
+                )
 
             @pl.when(c < LINE_FIRST)
             def _():
@@ -469,6 +523,20 @@
                     merge(c, line, wide, db)
                     d_copy(c, line, wide).start()
 
+        def ready(k):
+            @pl.when(s < STEPS - 1)
+            def _():
+                for half in range(halves):
+                    prepare(k + half * parts)
+
+                @pl.when(k < GROUP)
+                def _():
+                    send_own(k)
+
+                @pl.when(k == both % parts)
+                def _():
+                    h_copy(both, o, i, h_part, partner).start()
+
         def finish(c, wide):
             part = pl.ds(pl.multiple_of(c * sw, sw), sw)
 
@@ -487,10 +555,11 @@
             else:
                 out[:, part] += step_size * pb[c, o, i].astype(F32)
 
-                @pl.when(jnp.logical_and(s < STEPS - 1, c % per_gather == per_gather - 1))
-                def _():
-                    prepare(c // per_gather)
-                    send_own(c // per_gather)
+                @pl.when(
+                    jnp.logical_and(c >= per_gather, c % per_gather == per_gather - 1)
+                )
+                def _():
+                    ready(c // per_gather)
 
         def tick(at):
             @pl.when(jnp.logical_and(at >= LINE_FIRST, at < SCATTER_CHUNKS))
@@ -530,11 +599,7 @@
             @pl.when(at == SCATTER_CHUNKS)
             def _():
                 loop(LINE_FIRST, finish_wide)
-
-                @pl.when(s < STEPS - 1)
-                def _():
-                    prepare(both)
-                    h_copy(both, o, i, h_part, partner).start()
+                ready(0)
 
         loop(SCATTER_CHUNKS + lines - 1, tick_all)
 
@@ -563,24 +628,29 @@
 
         loop(SCATTER_CHUNKS, scatter_sends)
         for h in range(heads):
-
-            @pl.when(core == 0)
-            def _():
-                kv_copy(s, t, h, kv_sib.at[h], sibling).wait_send()
-
-            def chip_sends(other):
-                @pl.when(other > ch)
-                def _():
-                    kv_copy(s, t, h, kv_chip.at[h, other], other * 2 + core).wait_send()
-
-                @pl.when(other < ch)
-                def _():
-                    kv_copy(s, other * 2 + core, h, kv_fwd.at[h, other], sibling).wait_send()
-
-            loop(chips, chip_sends)
+            for half in range(halves):
+
+                @pl.when(core == 0)
+                def _():
+                    kv_copy(s, t, h, half, kv_sib.at[h], sibling).wait_send()
+
+                def chip_sends(other):
+                    @pl.when(other > ch)
+                    def _():
+                        kv_copy(
+                            s, t, h, half, kv_chip.at[h, other], other * 2 + core
+                        ).wait_send()
+
+                    @pl.when(other < ch)
+                    def _():
+                        kv_copy(
+                            s, other * 2 + core, h, half, kv_fwd.at[h, other], sibling
+                        ).wait_send()
+
+                loop(chips, chip_sends)
 
     h_copy(both, o, i, h_part, partner).start()
-    for c in range(1, GATHER_CHUNKS):
+    for c in range(GROUP):
         send_own(c)
     r_forward(o, True, True)
     loop(STEPS, step)
@@ -593,7 +663,8 @@
     heads = head_cols // HD
     seg = rows * tp_count
     lines, chips = tp_count // 2, tm_count // 2
-    gw, sw = width // GATHER_CHUNKS, width // SCATTER_CHUNKS
+    halves = halves_of(rows)
+    gw, sw = width * halves // GATHER_CHUNKS, width // SCATTER_CHUNKS
     dma = pltpu.SemaphoreType.DMA
     vmem = pl.BlockSpec(memory_space=pltpu.VMEM)
     smem = pl.BlockSpec(memory_space=pltpu.SMEM)
@@ -607,11 +678,11 @@
         scratch_shapes=[
             pltpu.VMEM((3, width, head_cols), BF16),
             pltpu.VMEM((head_cols, width), BF16),
-            pltpu.VMEM((g, lines, 2, rows, gw), BF16),
+            pltpu.VMEM((g, lines, 2, rows // halves, gw), BF16),
             pltpu.VMEM((lines, 2, 8, HD), F32),
-            pltpu.VMEM((3, seg, head_cols), F32),
+            pltpu.VMEM((halves, 3, seg // halves, head_cols), F32),
             pltpu.VMEM((heads, seg, HD), BF16),
-            pltpu.VMEM((STEPS, tm_count, heads, 2, seg, HD), BF16),
+            pltpu.VMEM((STEPS, tm_count, heads, halves, 2, seg // halves, HD), BF16),
             pltpu.VMEM((seg, head_cols), BF16),
             pltpu.VMEM((heads, seg, HD), F32),
             pltpu.VMEM((heads, seg, 2 * HD), F32),
@@ -619,7 +690,7 @@
             pltpu.VMEM((s, lines, rows, sw), BF16),
             pltpu.VMEM((s, lines, 2, rows, sw), BF16),
             pltpu.VMEM((s, lines, 2, rows, sw), BF16),
-            dma((g,)),
+            dma((width // gw,)),
             dma,
             dma((g, lines, 2)),
             dma((g, lines, 2)),
@@ -629,10 +700,10 @@
             dma((lines,)),
             dma((lines,)),
             dma((lines,)),
-            dma((STEPS, tm_count, heads)),
-            dma((heads,)),
-            dma((heads, chips)),
-            dma((heads, chips)),
+            dma((STEPS, tm_count, heads, halves)),
+            dma((heads, halves)),
+            dma((heads, chips, halves)),
+            dma((heads, chips, halves)),
             dma((s,)),
             dma((s,)),
             dma((s, lines)),

time: 178 us -> 175 us (0.983)
  Pallas kernels: 175 us -> 173 us
    pallas_call x1, Pallas kernels: 175 us -> 173 us  [shards(): pl.pallas_call(functools.partial(kernel, tm_count, tp_count), out_shape=j...]
where the time goes in v4:
time: 175 us
  Pallas kernels  173 us (99%)
  local copies, waits for them, and re-layouts  2.06 us (1%)
    pallas_call x1, Pallas kernels, shards(): pl.pallas_call(functools.partial(kernel, tm_count, tp_count), out_shape=j...  173 us

profile of v4, /device:TPU:2, one launch (start us, length us, event | category | flops | bytes accessed | tf_op | source)
XLA Modules:
  0.0 174.7 jit_solution(18021961503858642379)
XLA Ops:
  0.0 172.7 %shard_map.64 = f32[32,6144]{1,0:T(8,128)} custom-call(f32[32,6144]{1,0:T(8,128)} %states.1, f32[1,6144]{1,0:T(1,128)} %bitcast.3, bf16[3,6144,512]{2,1,0:T(8,128)(2,1)} %bitcast.2, f32[2,512]{1,0:T(2,128)} %qk_gain.1, bf16[512,6144]{1,0:T(8,128)(2,1)} %wo_hbm.1, s32[4]{0:T(128)} %lengths.1), custom_call_target="tpu_custom_call" | custom-call | flops 12884901888 | bytes 25165824 | tf_op jit(solution)/shard_map/pallas_call | solution.py:673
  172.7 2.1 %copy.8 = f32[32,6144]{1,0:T(8,128)} copy(f32[32,6144]{1,0:T(8,128)} %shard_map.64) | data formatting | bytes 1572864

commit v5 on v4

--- a/solution.py
+++ b/solution.py
@@ -380,10 +380,68 @@
         emit_keys(halves - 1)
         emit_queries(halves - 1)
 
-        @pl.when(core == 0)
+        def pass_on(pair, part):
+            def one(other):
+                @pl.when(other < ch)
+                def _():
+                    for h in pair:
+                        for half in part:
+                            got = kv_copy(
+                                s, other * 2 + core, h, half, kv_fwd.at[h, other], sibling
+                            )
+                            got.wait_recv()
+                            got.start()
+
+            loop(chips, one)
+
+        pass_on(range(heads), range(halves - 1))
+        for h in range(heads):
+            flash(s, h, [t], True)
+
+        @pl.when(s == 0)
         def _():
-            for h in range(heads):
-                flash(s, h, [t], True)
+            wo_copy.wait()
+
+        def gather_sends(c):
+            def one(line):
+                h_copy(c, line, i, h_part, partner).wait_send()
+                way_sends(c, line, i)
+
+            loop(lines, one)
+
+        def scale_sends(line):
+            r_copy(line, i, r_part, partner).wait_send()
+
+            @pl.when(jnp.logical_and(has_above, line <= o))
+            def _():
+                r_copy(line, i, r_up, above).wait_send()
+
+            @pl.when(jnp.logical_and(has_below, line >= o))
+            def _():
+                r_copy(line, i, r_down, below).wait_send()
+
+        def way_sends(c, line, side):
+            @pl.when(jnp.logical_and(has_above, line <= o))
+            def _():
+                h_copy(c, line, side, h_up, above).wait_send()
+
+            @pl.when(jnp.logical_and(has_below, line >= o))
+            def _():
+                h_copy(c, line, side, h_down, below).wait_send()
+
+        def both_sends(line):
+            way_sends(both, line, i)
+            way_sends(both, line, 1 - i)
+
+        def chunk_sends(c):
+            @pl.when(c != both)
+            def _():
+                gather_sends(c)
+
+        loop(GATHER_CHUNKS, chunk_sends)
+        h_copy(both, o, i, h_part, partner).wait_send()
+        loop(lines, both_sends)
+        loop(lines, scale_sends)
 
         @pl.when(core == 1)
         def _():
@@ -391,75 +449,32 @@
                 for half in range(halves):
                     kv_copy(s, t - 1, h, half, kv_sib.at[h], sibling).wait_recv()
             for h in range(heads):
-                flash(s, h, [t, t - 1], True)
-
-        @pl.when(s == 0)
-        def _():
-            wo_copy.wait()
-
-        def gather_sends(c):
-            def one(line):
-                h_copy(c, line, i, h_part, partner).wait_send()
-                way_sends(c, line, i)
-
-            loop(lines, one)
-
-        def scale_sends(line):
-            r_copy(line, i, r_part, partner).wait_send()
-
-            @pl.when(jnp.logical_and(has_above, line <= o))
-            def _():
-                r_copy(line, i, r_up, above).wait_send()
-
-            @pl.when(jnp.logical_and(has_below, line >= o))
-            def _():
-                r_copy(line, i, r_down, below).wait_send()
-
-        def way_sends(c, line, side):
-            @pl.when(jnp.logical_and(has_above, line <= o))
-            def _():
-                h_copy(c, line, side, h_up, above).wait_send()
-
-            @pl.when(jnp.logical_and(has_below, line >= o))
-            def _():
-                h_copy(c, line, side, h_down, below).wait_send()
-
-        def both_sends(line):
-            way_sends(both, line, i)
-            way_sends(both, line, 1 - i)
-
-        def chunk_sends(c):
-            @pl.when(c != both)
-            def _():
-                gather_sends(c)
-
-        loop(GATHER_CHUNKS, chunk_sends)
-        h_copy(both, o, i, h_part, partner).wait_send()
-        loop(lines, both_sends)
-        loop(lines, scale_sends)
-
-        for group in range(0, heads, 2):
-            pair = range(group, min(group + 2, heads))
-
-            def arrived(other):
+                flash(s, h, [t - 1], False)
+
+        pairs = [range(h, min(h + 2, heads)) for h in range(0, heads, 2)]
+        for pair in pairs:
+            pass_on(pair, range(halves - 1, halves))
+
+            def direct(other):
                 @pl.when(other < ch)
                 def _():
-                    g = other * 2 + core
-                    g_passed = other * 2 + 1 - core
+                    for h in pair:
+                        flash(s, h, [other * 2 + core], False)
+
+            loop(chips, direct)
+        for pair in pairs:
+
+            def passed(other):
+                @pl.when(other < ch)
+                def _():
+                    g = other * 2 + 1 - core
                     for h in pair:
                         for half in range(halves):
-                            got = kv_copy(s, g, h, half, kv_fwd.at[h, other], sibling)
-                            got.wait_recv()
-                            got.start()
+                            kv_copy(s, g, h, half, kv_fwd.at[h, other], sibling).wait_recv()
                     for h in pair:
-                        for half in range(halves):
-                            kv_copy(
-                                s, g_passed, h, half, kv_fwd.at[h, other], sibling
-                            ).wait_recv()
-                    for h in pair:
-                        flash(s, h, [g, g_passed], False)
-
-            loop(chips, arrived)
+                        flash(s, h, [g], False)
+
+            loop(chips, passed)
         for h in range(heads):
             att[:, h * HD : (h + 1) * HD] = (
                 run_acc[h][:, :HD] / run_acc[h][:, HD:]

time: 175 us -> 174 us (level)
  no operation moved by 1% of the time
where the time goes in v5:
time: 174 us
  Pallas kernels  172 us (99%)
  local copies, waits for them, and re-layouts  2.06 us (1%)
    pallas_call x1, Pallas kernels, shards(): pl.pallas_call(functools.partial(kernel, tm_count, tp_count), out_shape=j...  172 us

profile of v5, /device:TPU:2, one launch (start us, length us, event | category | flops | bytes accessed | tf_op | source)
XLA Modules:
  0.0 174.3 jit_solution(10416978548797486116)
XLA Ops:
  0.0 172.2 %shard_map.64 = f32[32,6144]{1,0:T(8,128)} custom-call(f32[32,6144]{1,0:T(8,128)} %states.1, f32[1,6144]{1,0:T(1,128)} %bitcast.3, bf16[3,6144,512]{2,1,0:T(8,128)(2,1)} %bitcast.2, f32[2,512]{1,0:T(2,128)} %qk_gain.1, bf16[512,6144]{1,0:T(8,128)(2,1)} %wo_hbm.1, s32[4]{0:T(128)} %lengths.1), custom_call_target="tpu_custom_call" | custom-call | flops 12884901888 | bytes 25165824 | tf_op jit(solution)/shard_map/pallas_call | solution.py:688
  172.2 2.1 %copy.8 = f32[32,6144]{1,0:T(8,128)} copy(f32[32,6144]{1,0:T(8,128)} %shard_map.64) | data formatting | bytes 1572864

commit v6 on v5

--- a/solution.py
+++ b/solution.py
@@ -12,8 +12,8 @@
 STEPS = 2
 GATHER_CHUNKS = 6
 GROUP = 3
-SCATTER_CHUNKS = 12
-LINE_FIRST = 2
+SCATTER_CHUNKS = 24
+LINE_FIRST = 4
 
 eps_norm = 1e-06
 step_size = -0.5

time: 174 us -> 208 us (1.20)
  Pallas kernels: 172 us -> 205 us
    pallas_call x1, Pallas kernels: 172 us -> 205 us  [shards(): pl.pallas_call(functools.partial(kernel, tm_count, tp_count), out_shape=j...]
where the time goes in v6:
time: 208 us; the launch traced here: 207 us
  Pallas kernels  205 us (99%)
    pallas_call x1, Pallas kernels, shards(): pl.pallas_call(functools.partial(kernel, tm_count, tp_count), out_shape=j...  205 us

profile of v6, /device:TPU:2, one launch (start us, length us, event | category | flops | bytes accessed | tf_op | source)
XLA Modules:
  0.0 207.5 jit_solution(11244716835026320780)
XLA Ops:
  0.0 205.4 %shard_map.64 = f32[32,6144]{1,0:T(8,128)} custom-call(f32[32,6144]{1,0:T(8,128)} %states.1, f32[1,6144]{1,0:T(1,128)} %bitcast.3, bf16[3,6144,512]{2,1,0:T(8,128)(2,1)} %bitcast.2, f32[2,512]{1,0:T(2,128)} %qk_gain.1, bf16[512,6144]{1,0:T(8,128)(2,1)} %wo_hbm.1, s32[4]{0:T(128)} %lengths.1), custom_call_target="tpu_custom_call" | custom-call | flops 12884901888 | bytes 25165824 | tf_op jit(solution)/shard_map/pallas_call | solution.py:688
  205.4 2.1 copy.8

commit v7 on v6

--- a/solution.py
+++ b/solution.py
@@ -12,8 +12,8 @@
 STEPS = 2
 GATHER_CHUNKS = 6
 GROUP = 3
-SCATTER_CHUNKS = 24
-LINE_FIRST = 4
+SCATTER_CHUNKS = 6
+LINE_FIRST = 1
 
 eps_norm = 1e-06
 step_size = -0.5

time: 208 us -> 177 us (0.85)
  Pallas kernels: 205 us -> 175 us
    pallas_call x1, Pallas kernels: 205 us -> 175 us  [shards(): pl.pallas_call(functools.partial(kernel, tm_count, tp_count), out_shape=j...]
where the time goes in v7:
time: 177 us
  Pallas kernels  175 us (99%)
  local copies, waits for them, and re-layouts  2.06 us (1%)
    pallas_call x1, Pallas kernels, shards(): pl.pallas_call(functools.partial(kernel, tm_count, tp_count), out_shape=j...  175 us

profile of v7, /device:TPU:2, one launch (start us, length us, event | category | flops | bytes accessed | tf_op | source)
XLA Modules:
  0.0 176.7 jit_solution(14207727893339324520)
XLA Ops:
  0.0 174.6 %shard_map.64 = f32[32,6144]{1,0:T(8,128)} custom-call(f32[32,6144]{1,0:T(8,128)} %states.1, f32[1,6144]{1,0:T(1,128)} %bitcast.3, bf16[3,6144,512]{2,1,0:T(8,128)(2,1)} %bitcast.2, f32[2,512]{1,0:T(2,128)} %qk_gain.1, bf16[512,6144]{1,0:T(8,128)(2,1)} %wo_hbm.1, s32[4]{0:T(128)} %lengths.1), custom_call_target="tpu_custom_call" | custom-call | flops 12884901888 | bytes 25165824 | tf_op jit(solution)/shard_map/pallas_call | solution.py:688
  174.6 2.1 %copy.8 = f32[32,6144]{1,0:T(8,128)} copy(f32[32,6144]{1,0:T(8,128)} %shard_map.64) | data formatting | bytes 1572864

commit v8 on v5

--- a/solution.py
+++ b/solution.py
@@ -228,16 +228,18 @@
     def rows_of(buffer, c, line, wide):
         return buffer.at[c, line] if wide else buffer.at[c, line, i]
 
-    def u_copy(c, line, wide):
+    def u_copy(c, k, wide):
+        lines_on = pl.ds(k + 1, lines - 1 - k)
         return remote(
-            rows_of(pb, c, line, wide), rows_of(ub, c, line, wide),
-            u_send.at[c, line], u_recv.at[c, line], t, above,
+            rows_of(pb, c, lines_on, wide), rows_of(ub, c, lines_on, wide),
+            u_send.at[c, 0], u_recv.at[c, 0], t, above,
         )
 
-    def d_copy(c, line, wide):
+    def d_copy(c, k, wide):
+        lines_on = pl.ds(0, k)
         return remote(
-            rows_of(pb, c, line, wide), rows_of(db, c, line, wide),
-            d_send.at[c, line], d_recv.at[c, line], t, below,
+            rows_of(pb, c, lines_on, wide), rows_of(db, c, lines_on, wide),
+            d_send.at[c, 0], d_recv.at[c, 0], t, below,
         )
 
     def step(s):
@@ -501,13 +503,11 @@
         def start_line(c, wide):
             @pl.when(o == 0)
             def _():
-                for line in range(lines - 1, 0, -1):
-                    u_copy(c, line, wide).start()
+                u_copy(c, 0, wide).start()
 
             @pl.when(o == lines - 1)
             def _():
-                for line in range(lines - 1):
-                    d_copy(c, line, wide).start()
+                d_copy(c, lines - 1, wide).start()
 
         loop(SCATTER_CHUNKS, partial)
 
@@ -520,23 +520,17 @@
             mine, theirs = rows_of(pb, c, line, wide), rows_of(buffer, c, line, wide)
             mine[...] = (mine[...].astype(F32) + theirs[...].astype(F32)).astype(BF16)
 
-        def hop(c, wide):
-            for line in range(lines - 1, 0, -1):
-
-                @pl.when(line > o)
-                def _():
-                    u_copy(c, line, wide).wait_recv()
-                    merge(c, line, wide, ub)
-                    u_copy(c, line, wide).start()
-
-        def hop_down(c, wide):
-            for line in range(lines - 1):
-
-                @pl.when(line < o)
-                def _():
-                    d_copy(c, line, wide).wait_recv()
-                    merge(c, line, wide, db)
-                    d_copy(c, line, wide).start()
+        def hop(c, k, wide):
+            u_copy(c, k - 1, wide).wait_recv()
+            for line in range(k + 1, lines):
+                merge(c, line, wide, ub)
+            u_copy(c, k, wide).start()
+
+        def hop_down(c, k, wide):
+            d_copy(c, k + 1, wide).wait_recv()
+            for line in range(k):
+                merge(c, line, wide, db)
+            d_copy(c, k, wide).start()
 
         def ready(k):
             @pl.when(s < STEPS - 1)
@@ -555,14 +549,20 @@
         def finish(c, wide):
             part = pl.ds(pl.multiple_of(c * sw, sw), sw)
 
+            @pl.when(o == lines - 1)
+            def _():
+                u_copy(c, lines - 2, wide).wait_recv()
+
+            @pl.when(o == 0)
+            def _():
+                d_copy(c, 1, wide).wait_recv()
+
             @pl.when(has_below)
             def _():
-                u_copy(c, o, wide).wait_recv()
                 merge(c, o, wide, ub)
 
             @pl.when(has_above)
             def _():
-                d_copy(c, o, wide).wait_recv()
                 merge(c, o, wide, db)
 
             if wide:
@@ -592,11 +592,11 @@
 
                         @pl.when(jnp.logical_and(live, o == k))
                         def _():
-                            hop(c, wide)
+                            hop(c, k, wide)
 
                         @pl.when(jnp.logical_and(live, lines - 1 - o == k))
                         def _():
-                            hop_down(c, wide)
+                            hop_down(c, lines - 1 - k, wide)
                     else:
 
                         @pl.when(live)
@@ -630,16 +630,14 @@
                 def _():
                     (y_copy_wide if wide else y_copy)(c).wait_send()
 
-                    def one(line):
-                        @pl.when(jnp.logical_and(has_above, line > o))
+                    for k in range(lines):
+
+                        @pl.when(o == k)
                         def _():
-                            u_copy(c, line, wide).wait_send()
-
-                        @pl.when(jnp.logical_and(has_below, line < o))
-                        def _():
-                            d_copy(c, line, wide).wait_send()
-
-                    loop(lines, one)
+                            if k < lines - 1:
+                                u_copy(c, k, wide).wait_send()
+                            if k > 0:
+                                d_copy(c, k, wide).wait_send()
 
         loop(SCATTER_CHUNKS, scatter_sends)
         for h in range(heads):

time: 174 us -> 182 us (1.046)
  Pallas kernels: 172 us -> 180 us
    pallas_call x1, Pallas kernels: 172 us -> 180 us  [shards(): pl.pallas_call(functools.partial(kernel, tm_count, tp_count), out_shape=j...]
where the time goes in v8:
time: 182 us
  Pallas kernels  180 us (99%)
  local copies, waits for them, and re-layouts  2.06 us (1%)
    pallas_call x1, Pallas kernels, shards(): pl.pallas_call(functools.partial(kernel, tm_count, tp_count), out_shape=j...  180 us

profile of v8, /device:TPU:2, one launch (start us, length us, event | category | flops | bytes accessed | tf_op | source)
XLA Modules:
  0.0 182.2 jit_solution(12288360425596012120)
XLA Ops:
  0.0 180.1 %shard_map.64 = f32[32,6144]{1,0:T(8,128)} custom-call(f32[32,6144]{1,0:T(8,128)} %states.1, f32[1,6144]{1,0:T(1,128)} %bitcast.3, bf16[3,6144,512]{2,1,0:T(8,128)(2,1)} %bitcast.2, f32[2,512]{1,0:T(2,128)} %qk_gain.1, bf16[512,6144]{1,0:T(8,128)(2,1)} %wo_hbm.1, s32[4]{0:T(128)} %lengths.1), custom_call_target="tpu_custom_call" | custom-call | flops 12884901888 | bytes 25165824 | tf_op jit(solution)/shard_map/pallas_call | solution.py:686
  180.1 2.1 %copy.8 = f32[32,6144]{1,0:T(8,128)} copy(f32[32,6144]{1,0:T(8,128)} %shard_map.64) | data formatting | bytes 1572864
